TPU v7x, 128 devices: a whole 4x4x4 slice. The times are simulated.
128 devices in a mesh: segment: 4 (over z), space: 32 (over y, x, core).
Axes of the slice: x: 4, y: 4, z: 4, core: 2. Of those that a mesh axis runs over, the one named last changes fastest.
Arguments:
- text_states: bfloat16 [2, 32, 128, 4096], P(None, 'space'), may hold values from -6 to 6
- token_ids: int32 [2, 32, 128], replicated, may hold values from 0 to 32127, as said below
- step_ids: int32 [3, 2], replicated, may hold values from 100 to 899
- base_noise: bfloat16 [2, 32, 3, 1024], P(None, 'space'), may hold values from -6 to 6
- upscale_noise: bfloat16 [2, 32, 3, 1024], P(None, 'space'), may hold values from -6 to 6
- final_noise: bfloat16 [2, 32, 3, 512, 32], P(None, None, None, 'space'), may hold values from -6 to 6
- t5_gain: float32 [4096], replicated, may hold values from 0.5 to 1.5
- base_keyval: bfloat16 [4096, 1024], replicated, may hold values from -0.09375 to 0.09375
- upscale_keyval: bfloat16 [2, 4096, 256], replicated, may hold values from -0.09375 to 0.09375
- base_input: bfloat16 [3, 512], replicated, may hold values from -3.5 to 3.5
- base_time: bfloat16 [512, 512], replicated, may hold values from -0.25 to 0.25
- base_gain: float32 [3, 512], replicated, may hold values from 0.5 to 1.5
- base_conv: bfloat16 [9, 512, 512], replicated, may hold values from -0.09375 to 0.09375
- base_query: bfloat16 [512, 512], replicated, may hold values from -0.25 to 0.25
- base_output: bfloat16 [512, 512], replicated, may hold values from -0.25 to 0.25
- base_head: bfloat16 [512, 3], replicated, may hold values from -0.25 to 0.25
- upscale_input: bfloat16 [2, 6, 128], replicated, may hold values from -2.5 to 2.5
- upscale_time: bfloat16 [2, 128, 128], replicated, may hold values from -0.5 to 0.5
- upscale_gain: float32 [2, 3, 128], replicated, may hold values from 0.5 to 1.5
- upscale_conv: bfloat16 [2, 9, 128, 128], replicated, may hold values from -0.1875 to 0.1875
- upscale_query: bfloat16 [2, 128, 128], replicated, may hold values from -0.5 to 0.5
- upscale_output: bfloat16 [2, 128, 128], replicated, may hold values from -0.5 to 0.5
- upscale_head: bfloat16 [2, 128, 3], replicated, may hold values from -0.5 to 0.5
Outputs:
- early_states: bfloat16 [2, 2, 32, 3, 1024], P(None, None, 'space', None, 'segment')
- final_states: bfloat16 [2, 2, 32, 3, 512, 32], P(None, None, 'segment', None, 'space')
Inputs may be any that keep to these rules, and one draw needn't show every extreme that they name: `token_ids`: each prompt's ids are nonzero on its first 1 to 128 positions and 0 (padding) after them; some prompt fills all 128 positions.
All inputs are finite; a program needn't handle non-finite values.
Results may differ from a plain program's by a relative error of at most 0.0095.
Values may be sent and summed in bfloat16 or wider, within the bound.
A program may use at most 256 MiB of HBM per device.

v0:
```python
import functools
import math

import jax
import jax.numpy as jnp
from jax import lax
from jax.experimental import pallas as pl
from jax.experimental.pallas import tpu as pltpu
from jax.sharding import PartitionSpec as P

MESH = pl.DeviceIdType.MESH
ANY = pl.BlockSpec(memory_space=pl.ANY)
VMEM = pl.BlockSpec(memory_space=pltpu.VMEM)
SMEM = pl.BlockSpec(memory_space=pltpu.SMEM)
F32, BF16 = jnp.float32, jnp.bfloat16
LOG2E = 1.4426950408889634
SCALE = 0.125 * LOG2E
SEG, LANE = 4, 8
STEPS = 4


def dot(a, b):
    return jnp.dot(a, b, preferred_element_type=F32)


def dot_nt(a, b):
    return lax.dot_general(a, b, (((1,), (1,)), ((), ())), preferred_element_type=F32)


def iota(shape, dim):
    return lax.broadcasted_iota(jnp.int32, shape, dim)


def place():
    z = lax.axis_index("segment")
    p = lax.axis_index("space")
    return z, p // LANE, p % LANE


def remote(src, dst, send, recv, z, p):
    return pltpu.make_async_remote_copy(
        src_ref=src, dst_ref=dst, send_sem=send, recv_sem=recv, device_id=(z, p), device_id_type=MESH
    )


def gather_kernel(noise, got, send, recv, halo_send, own_sem):
    z, y, k = place()
    barrier = pltpu.get_barrier_semaphore()
    for j in range(LANE):
        @pl.when((y != z) | (k != j))
        def _():
            pl.semaphore_signal(barrier, inc=1, device_id=(y, z * LANE + j), device_id_type=MESH)

    @pl.when(z > 0)
    def _():
        pl.semaphore_signal(barrier, inc=1, device_id=(y, z * LANE - 1), device_id_type=MESH)

    @pl.when(z < SEG - 1)
    def _():
        pl.semaphore_signal(barrier, inc=1, device_id=(y, z * LANE + LANE), device_id_type=MESH)

    lower = (k == LANE - 1) & (y < SEG - 1)
    upper = (k == 0) & (y > 0)
    extra = jnp.where(lower | upper, LANE, 0)
    pl.semaphore_wait(barrier, LANE - 1 + jnp.where(y != z, 1, 0) + extra)

    def main(j):
        return remote(noise.at[:, z * LANE + j], got.at[k], send.at[j], recv.at[k], y, z * LANE + j)

    def halo(j, slot, to):
        return remote(noise.at[:, z * LANE + j], got.at[slot], halo_send.at[j], recv.at[slot], to, z * LANE + j)

    own = pltpu.make_async_copy(noise.at[:, z * LANE + k], got.at[k], own_sem)
    for j in range(LANE):
        @pl.when((y != z) | (k != j))
        def _():
            main(j).start()

    @pl.when(y == z)
    def _():
        own.start()

    for cond, slot, step in ((lower, LANE, 1), (upper, LANE + 1, -1)):
        @pl.when(cond)
        def _():
            for j in range(LANE):
                halo(j, slot, y + step).start()

    for j in range(LANE):
        @pl.when((y != z) | (k != j))
        def _():
            main(j).wait_send()
            remote(noise.at[:, z * LANE + j], got.at[j], send.at[j], recv.at[j], y, z * LANE + j).wait_recv()

    @pl.when(y == z)
    def _():
        own.wait()

    for cond, slot, step in ((lower, LANE, 1), (upper, LANE + 1, -1)):
        @pl.when(cond)
        def _():
            for j in range(LANE):
                halo(j, slot, y + step).wait_send()

    @pl.when(z > 0)
    def _():
        halo(0, LANE, y).wait_recv()

    @pl.when(z < SEG - 1)
    def _():
        halo(0, LANE + 1, y).wait_recv()


def scatter_kernel(parts, out, send, recv, own_sem):
    z, y, k = place()
    barrier = pltpu.get_barrier_semaphore()
    for j in range(LANE):
        @pl.when((y != z) | (k != j))
        def _():
            pl.semaphore_signal(barrier, inc=1, device_id=(y, z * LANE + j), device_id_type=MESH)
    pl.semaphore_wait(barrier, LANE - 1 + jnp.where(y != z, 1, 0))

    def main(j):
        return remote(parts.at[j], out.at[:, :, k], send.at[j], recv.at[k], y, z * LANE + j)

    own = pltpu.make_async_copy(parts.at[k], out.at[:, :, k], own_sem)
    for j in range(LANE):
        @pl.when((y != z) | (k != j))
        def _():
            main(j).start()

    @pl.when(y == z)
    def _():
        own.start()

    for j in range(LANE):
        @pl.when((y != z) | (k != j))
        def _():
            main(j).wait_send()
            remote(parts.at[j], out.at[:, :, j], send.at[j], recv.at[j], y, z * LANE + j).wait_recv()

    @pl.when(y == z)
    def _():
        own.wait()


def work_kernel(
    coef, ids, bx, ux, eb, eu, t5g, b_in, b_gain, b_head, u_in, u_gain, u_head,
    text_h, bkv_h, ukv_h, btime_h, bconv_h, bq_h, bo_h, utime_h, uconv_h, uq_h, uo_h, noise_h,
    early, parts,
    text_v, kv_w, btime_v, bconv_v, bq_v, bo_v, utime_v, uconv_v, uq_v, uo_v, noise_v,
    ctx, kv, taps, hid, query, att, x8b, x8u, rows8, aug8, gcol, wq_t, wo_t, wh_t, conv_t,
    kcat, vcat, mask_row, mask_col, head8, x2, hid3, act3, c2, sems,
):
    z, y, k = place()
    p = y * LANE + k

    copies = [
        pltpu.make_async_copy(src, dst, sems.at[n])
        for n, (src, dst) in enumerate(
            [
                (utime_h, utime_v), (uq_h, uq_v), (uo_h, uo_v), (uconv_h, uconv_v), (btime_h, btime_v),
                (bconv_h, bconv_v), (text_h, text_v),
            ]
            + [(bkv_h.at[:, 256 * n : 256 * n + 256], kv_w.at[n]) for n in range(4)]
            + [(ukv_h.at[n], kv_w.at[4 + n]) for n in range(2)]
            + [(bq_h, bq_v), (bo_h, bo_v), (noise_h, noise_v)]
        )
    ]
    for copy in copies:
        copy.start()
    at = dict(utime=0, uq=1, uo=2, uconv=3, btime=4, bconv=5, text=6, kv=7, bq=13, bo=14, noise=15)

    lane128 = iota((128, 128), 1)
    sub128 = iota((128, 128), 0)
    for m in range(2):
        x8b[m] = jnp.zeros((8, 1024), F32)
        x8u[m] = jnp.zeros((8, 1024), F32)
        x8b[m, 0:3, :] = bx[m].astype(F32)
        x8u[m, 0:3, :] = ux[m].astype(F32)
        row = jnp.where(ids[m, pl.ds(p, 1), :] != 0, 0.0, -1e30)
        mask_row[m, :, 0:128] = row
        mask_row[m, :, 128:256] = row
        rows8[...] = jnp.broadcast_to(row, (8, 128))
        column = jnp.transpose(rows8[...])[:, 0:1]
        mask_col[m] = jnp.broadcast_to(column, (128, 128))
    head8[...] = jnp.zeros_like(head8)
    head8[0:3, :] = b_head[...].astype(F32)

    for n in range(4):
        copies[n].wait()
    for s in range(2):
        emb = dot(eu[...].astype(BF16), utime_v[s])
        for m in range(2):
            aug8[0:6, :] = u_in[s].astype(F32)
            one = emb[2 * s + m : 2 * s + m + 1, :]
            high = one.astype(BF16).astype(F32)
            aug8[6:7, :] = high
            aug8[7:8, :] = one - high
            x8 = jnp.transpose(aug8[...]).astype(BF16)
            gcol[2 + 2 * s + m, :, 0:8] = x8.astype(F32)
        rows8[...] = jnp.zeros((8, 128), F32)
        rows8[0:3, :] = u_gain[s]
        turned = jnp.transpose(rows8[...])
        gcol[s] = jnp.broadcast_to(turned[:, 0:1] * 0.5, (128, 128))
        wq_t[s] = jnp.transpose(uq_v[s].astype(F32) * (turned[:, 1:2] * SCALE)).astype(BF16)
        wo_t[s] = jnp.transpose(uo_v[s].astype(F32)).astype(BF16)
        rows8[...] = jnp.zeros((8, 128), F32)
        rows8[0:3, :] = u_head[s].astype(F32) * u_gain[s, 2:3, :]
        wh_t[s] = rows8[...].astype(BF16)
        for tap in range(9):
            conv_t[s, :, 128 * tap : 128 * tap + 128] = jnp.transpose(uconv_v[s, tap].astype(F32)).astype(BF16)

    copies[at["btime"]].wait()
    emb_b = dot(eb[...].astype(BF16), btime_v[...])
    w_in = b_in[...]
    for m in range(2):
        rolled = pltpu.roll(x8b[m], jnp.mod(32 - 256 * z, 1024), 1)
        own_t = jnp.transpose(rolled[:, 0:384])[0:320, :]
        blk_t = jnp.transpose(x8b[m, :, 0:384])[0:288, :].reshape(9, 32, 8)[:, 0:16, :].reshape(144, 8)
        pix = jnp.concatenate([own_t, blk_t], axis=0)[:, 0:3].astype(BF16)
        hidden = dot(pix, w_in) + emb_b[m : m + 1, :]
        scale = lax.rsqrt(jnp.mean(hidden * hidden, axis=-1, keepdims=True) + 1e-6)
        half = hidden * scale * (b_gain[0:1, :] * 0.5)
        active = half + half * jnp.tanh(half)
        hid[256 * m : 256 * m + 256, :] = hidden[32:288]
        hid[512 + 64 * m : 576 + 64 * m, :] = hidden[320:464].reshape(9, 16, 512)[0:8, 0:8].reshape(64, 512)
        own = active[0:320]
        line = iota((320, 1), 0)
        gone = ((line < 32) & (z == 0)) | ((line >= 288) & (z == SEG - 1))
        own = jnp.where(gone, 0.0, own)
        blk = active[320:464]
        col = line % 32
        bcol = iota((144, 1), 0) % 16
        for b in range(3):
            if b == 0:
                mine = jnp.where(col == 0, 0.0, pltpu.roll(own, 1, 0))
                near = jnp.where(bcol == 0, 0.0, pltpu.roll(blk, 1, 0))
            elif b == 1:
                mine, near = own, blk
            else:
                mine = jnp.where(col == 31, 0.0, pltpu.roll(own, 319, 0))
                near = pltpu.roll(blk, 143, 0)
            mine = mine.astype(BF16)
            near = near.reshape(9, 16, 512)[:, 0:8].reshape(72, 512)
            near = jnp.concatenate([jnp.zeros((8, 512), F32), near], axis=0)
            for a in range(3):
                taps[3 * a + b, 256 * m : 256 * m + 256, :] = mine[32 * a : 32 * a + 256]
                taps[3 * a + b, 512 + 64 * m : 576 + 64 * m, :] = near[8 * a : 8 * a + 64].astype(BF16)

    copies[at["bconv"]].wait()

    def conv_step(tap, carry):
        hid[...] += dot(taps[tap], bconv_v[tap])
        return carry

    lax.fori_loop(0, 9, conv_step, 0)

    copies[at["text"]].wait()

    def norm_step(i, carry):
        at_row = pl.multiple_of(i * 32, 32)
        states = text_v[pl.ds(at_row, 32), :].astype(F32)
        scale = lax.rsqrt(jnp.mean(states * states, axis=-1, keepdims=True) + 1e-6)
        ctx[pl.ds(at_row, 32), :] = (states * scale * t5g[...]).astype(BF16)
        return carry

    lax.fori_loop(0, 8, norm_step, 0)
    for n in range(6):
        copies[at["kv"] + n].wait()
        kv[:, 256 * n : 256 * n + 256] = dot(ctx[...], kv_w[n]).astype(BF16)

    for s in range(2):
        for m in range(2):
            key = kv[128 * m : 128 * m + 128, 1024 + 256 * s : 1152 + 256 * s]
            val = jnp.transpose(kv[128 * m : 128 * m + 128, 1152 + 256 * s : 1280 + 256 * s].astype(F32)).astype(BF16)
            zero = jnp.zeros_like(key)
            kcat[2 * s + m, 0:128, :] = jnp.where(lane128 < 64, key, zero)
            kcat[2 * s + m, 128:256, :] = jnp.where(lane128 < 64, zero, key)
            vcat[2 * s + m, 0:128, 0:128] = jnp.where(sub128 < 64, val, zero)
            vcat[2 * s + m, 0:128, 128:256] = jnp.where(sub128 < 64, zero, val)
            head_of = iota((16, 256), 1) // 128
            vcat[2 * s + m, 128:144, :] = (head_of == iota((16, 256), 0)).astype(F32).astype(BF16)

    copies[at["bq"]].wait()
    copies[at["bo"]].wait()
    h2 = hid[...]
    scale = lax.rsqrt(jnp.mean(h2 * h2, axis=-1, keepdims=True) + 1e-6)
    query[...] = (dot((h2 * scale * b_gain[1:2, :]).astype(BF16), bq_v[...]) * SCALE).astype(BF16)
    for m in range(2):
        for pair in range(4):
            lo = 128 * pair
            key = kv[128 * m : 128 * m + 128, lo : lo + 128]
            val = kv[128 * m : 128 * m + 128, 512 + lo : 640 + lo]
            zero = jnp.zeros_like(key)
            keys = jnp.concatenate([jnp.where(lane128 < 64, key, zero), jnp.where(lane128 < 64, zero, key)], axis=0)
            vals = jnp.concatenate([jnp.where(lane128 < 64, val, zero), jnp.where(lane128 < 64, zero, val)], axis=0)
            ones = ((iota((256, 128), 0) < 128) == (iota((256, 128), 1) < 64)).astype(F32).astype(BF16)
            vals = jnp.concatenate([vals, ones], axis=1)
            q = jnp.concatenate(
                [query[256 * m : 256 * m + 256, lo : lo + 128], query[512 + 64 * m : 576 + 64 * m, lo : lo + 128]], axis=0
            )
            score = dot_nt(q, keys) + mask_row[m]
            left, right = score[:, 0:128], score[:, 128:256]
            left = jnp.exp2(left - jnp.max(left, axis=-1, keepdims=True))
            right = jnp.exp2(right - jnp.max(right, axis=-1, keepdims=True))
            mixed = dot(jnp.concatenate([left, right], axis=1).astype(BF16), vals)
            mixed = (mixed[:, 0:128] / mixed[:, 128:256]).astype(BF16)
            att[256 * m : 256 * m + 256, lo : lo + 128] = mixed[0:256]
            att[512 + 64 * m : 576 + 64 * m, lo : lo + 128] = mixed[256:320]
    h3 = hid[...] + dot(att[...], bo_v[...])
    scale = lax.rsqrt(jnp.mean(h3 * h3, axis=-1, keepdims=True) + 1e-6)
    eps = dot_nt(head8[...].astype(BF16), (h3 * scale * b_gain[2:3, :]).astype(BF16))

    def step_of(noisy, eps, c0, c1, c2_, c3):
        clean = jnp.clip((noisy - c0 * eps) * c1, -1.0, 1.0)
        return clean, c2_ * clean + c3 * eps

    def coefs(s, m):
        return tuple(coef[(2 * s + m) * 4 + n] for n in range(4))

    pick_k, pick_l = iota((256, 128), 0), iota((256, 128), 1)
    noisy = jnp.zeros((8, 128), F32)
    for m in range(2):
        whole = pltpu.roll(x8b[m], jnp.mod(0 - 256 * z, 1024), 1)[:, 0:256]
        _, prior = step_of(whole, eps[:, 256 * m : 256 * m + 256], *coefs(0, m))
        early[0, m] = prior
        spot = pick_l - 64 * m
        sel = (spot >= 0) & (spot < 64) & (pick_k // 32 == spot // 8) & (pick_k % 32 == spot % 8)
        noisy += dot(x8b[m, :, 0:256].astype(BF16), sel.astype(F32).astype(BF16))
    first_half = iota((8, 128), 1) < 64
    mixed_coefs = tuple(jnp.where(first_half, a, b) for a, b in zip(coefs(0, 0), coefs(0, 1)))
    region, _ = step_of(noisy, eps[:, 512:640], *mixed_coefs)
    region = region.astype(BF16)

    def back(s, m, h2, width):
        sm = 2 * s + m
        scale = lax.rsqrt(jnp.sum(h2 * h2, axis=0, keepdims=True) * (1.0 / 128.0) + 1e-6)
        q = (dot(wq_t[s], h2.astype(BF16)) * scale).astype(BF16)
        score = dot(kcat[sm], q)
        mask = jnp.concatenate([mask_col[m]] * (width // 128), axis=1)
        left, right = score[0:128] + mask, score[128:256] + mask
        left = jnp.exp2(left - jnp.max(left, axis=0, keepdims=True)).astype(BF16)
        right = jnp.exp2(right - jnp.max(right, axis=0, keepdims=True)).astype(BF16)
        mixed = dot(vcat[sm], jnp.concatenate([left, right], axis=0))
        top = mixed[0:64] * (1.0 / mixed[128:129])
        bottom = mixed[64:128] * (1.0 / mixed[129:130])
        h3 = h2 + dot(wo_t[s], jnp.concatenate([top, bottom], axis=0).astype(BF16))
        scale = lax.rsqrt(jnp.sum(h3 * h3, axis=0, keepdims=True) * (1.0 / 128.0) + 1e-6)
        return dot(wh_t[s], h3.astype(BF16)) * scale

    def activate(hidden, s, width):
        scale = lax.rsqrt(jnp.sum(hidden * hidden, axis=0, keepdims=True) * (1.0 / 128.0) + 1e-6)
        gain = jnp.concatenate([gcol[s]] * (width // 128), axis=1)
        half = hidden * scale * gain
        return half + half * jnp.tanh(half)

    lanes = iota((1, 384), 1)
    row_of = 8 * z - 2 + lanes // 32
    col_of = lanes % 32
    inside = (row_of >= 0) & (row_of < 32)
    spread_k = iota((128, 384), 0)
    spread_l = iota((128, 384), 1)
    spread_at = ((8 * z - 2 + spread_l // 32 + 4) // 4 - 1) * 8 + (spread_l % 32) // 4
    for m in range(2):
        x = pltpu.roll(x8u[m], jnp.mod(64 - 256 * z, 1024), 1)[:, 0:384]
        sel = (spread_k == spread_at + 64 * m) & (spread_at >= 0) & (spread_at < 64)
        cond = dot(region, sel.astype(F32).astype(BF16))
        which = iota((8, 384), 0)
        cond = pltpu.roll(cond, 3, 0)
        x8 = jnp.where(which < 3, x, jnp.where(which < 6, cond, 1.0))
        hidden = dot(gcol[2 + m, :, 0:8].astype(BF16), x8.astype(BF16))
        active = jnp.where(inside, activate(hidden, 0, 384), 0.0)
        stack = [
            jnp.where(col_of == 0, 0.0, pltpu.roll(active, 1, 1)),
            active,
            jnp.where(col_of == 31, 0.0, pltpu.roll(active, 383, 1)),
        ]
        stack = [pltpu.roll(one, 32, 1) for one in stack] + stack + [pltpu.roll(one, 352, 1) for one in stack]
        stack = jnp.concatenate([one.astype(BF16) for one in stack], axis=0)
        h2 = hidden + dot(conv_t[0], stack)
        eps = back(0, m, h2, 384)
        clean, prior = step_of(x, eps, *coefs(1, m))
        early[1, m] = pltpu.roll(prior, 320, 1)[:, 0:256]
        clean = clean.astype(BF16)
        pick_k, pick_l = iota((384, 128), 0), iota((384, 128), 1)

        def rows_at(first):
            sel = (pick_k // 32 == first + 2 * (pick_l // 32)) & (pick_k % 32 == pick_l % 32)
            return dot(clean, sel.astype(F32).astype(BF16))

        x2[m] = jnp.ones((34 * 8, 128), F32)
        even, odd = rows_at(2), rows_at(3)
        above, below = rows_at(1), rows_at(4)
        for c in range(3):
            x2[m, pl.ds(8 + 3 + c, 16, 8), :] = jnp.broadcast_to(even[c : c + 1], (16, 128))
            x2[m, pl.ds(8 * 17 + 3 + c, 16, 8), :] = jnp.broadcast_to(odd[c : c + 1], (16, 128))
            x2[m, 3 + c : 4 + c, :] = above[c : c + 1]
            x2[m, 33 * 8 + 3 + c : 33 * 8 + 4 + c, :] = below[c : c + 1]

    copies[at["noise"]].wait()

    @pl.when(z == 0)
    def _():
        noise_v[8] = jnp.zeros((2, 3, 16, 32), BF16)

    @pl.when(z == SEG - 1)
    def _():
        noise_v[9] = jnp.zeros((2, 3, 16, 32), BF16)

    def spot(g):
        return (iota((32, 128), 0) + 32 * g == iota((32, 128), 1)).astype(F32).astype(BF16)

    lane1 = iota((1, 128), 1)
    for m in range(2):
        total = jnp.zeros((96, 128), F32)
        for g in range(4):
            pieces = jnp.concatenate([noise_v[2 * g, m], noise_v[2 * g + 1, m]], axis=1).reshape(96, 32)
            total += dot(pieces, spot(g))
        top = dot(noise_v[8, m].reshape(48, 32), spot(0))
        low = dot(noise_v[9, m].reshape(48, 32), spot(3))
        for c in range(3):
            one = total[32 * c : 32 * c + 32]
            x2[m, pl.ds(8 + c, 32, 8), :] = one
            x2[m, c : c + 1, :] = jnp.where(lane1 < 32, top[16 * c + 15 : 16 * c + 16], pltpu.roll(one[31:32], 32, 1))
            x2[m, 33 * 8 + c : 33 * 8 + c + 1, :] = jnp.where(
                lane1 >= 96, low[16 * c : 16 * c + 1], pltpu.roll(one[0:1], 96, 1)
            )

    lane2 = iota((1, 256), 1) % 128
    col2 = lane2 % 32
    for m in range(2):
        def front_step(n, carry):
            t = n * 2
            pair = x2[m, pl.ds(pl.multiple_of(t * 8, 16), 16), :]
            x8 = jnp.concatenate([pair[0:8], pair[8:16]], axis=1).astype(BF16)
            hidden = dot(gcol[4 + m, :, 0:8].astype(BF16), x8)
            hid3[t] = hidden[:, 0:128]
            hid3[t + 1] = hidden[:, 128:256]
            tile = t + iota((1, 256), 1) // 128
            gone = ((tile == 0) & (lane2 < 32) & (z == 0)) | ((tile == 33) & (lane2 >= 96) & (z == SEG - 1))
            active = jnp.where(gone, 0.0, activate(hidden, 1, 256))
            for h in range(2):
                one = active[:, 128 * h : 128 * h + 128]
                act3[t + h, 0:128] = jnp.where(col2[:, 0:128] == 0, 0.0, pltpu.roll(one, 1, 1)).astype(BF16)
                act3[t + h, 128:256] = one.astype(BF16)
                act3[t + h, 256:384] = jnp.where(col2[:, 0:128] == 31, 0.0, pltpu.roll(one, 127, 1)).astype(BF16)
            return carry

        lax.fori_loop(0, 17, front_step, 0)

        def back_step(n, carry):
            i = n * STEPS
            tiles = [act3[i + e] for e in range(STEPS + 2)]
            stack = jnp.concatenate(
                [jnp.concatenate(tiles[a : a + STEPS], axis=1) for a in range(3)], axis=0
            )
            h2 = jnp.concatenate([hid3[i + 1 + e] for e in range(STEPS)], axis=1) + dot(conv_t[1], stack)
            eps = back(1, m, h2, 128 * STEPS)
            rows = x2[m, pl.ds(pl.multiple_of((i + 1) * 8, 8), 8 * STEPS), :]
            noisy = jnp.concatenate([rows[8 * e : 8 * e + 8] for e in range(STEPS)], axis=1)
            clean, prior = step_of(noisy, eps, *coefs(2, m))
            for e in range(STEPS):
                spot_at = pl.ds(pl.multiple_of((i + e) * 8, 8), 8)
                c2[0, m, spot_at, :] = clean[:, 128 * e : 128 * e + 128]
                c2[1, m, spot_at, :] = prior[:, 128 * e : 128 * e + 128]
            return carry

        lax.fori_loop(0, 32 // STEPS, back_step, 0)

    everything = jnp.concatenate(
        [c2[o, m, pl.ds(c, 32, 8), :] for o in range(2) for m in range(2) for c in range(3)], axis=0
    ).astype(BF16)
    for g in range(4):
        sel = (iota((128, 32), 0) == iota((128, 32), 1) + 32 * g).astype(F32).astype(BF16)
        piece = dot(everything, sel).astype(BF16).reshape(2, 2, 3, 32, 32)
        parts[2 * g] = piece[:, :, :, 0:16]
        parts[2 * g + 1] = piece[:, :, :, 16:32]


def alpha_bar(step):
    frac = (step.astype(F32) / 1000.0 + 0.008) / 1.008
    return jnp.cos(frac * (math.pi / 2)) ** 2


def time_code(step, half):
    freqs = jnp.exp(-math.log(10000.0) * jnp.arange(half, dtype=F32) / half)
    angle = step.astype(F32)[:, None] * freqs
    return jnp.concatenate([jnp.sin(angle), jnp.cos(angle)], axis=1).astype(BF16).astype(F32)


def shards(
    text_states, token_ids, step_ids, base_noise, upscale_noise, final_noise, t5_gain,
    base_keyval, upscale_keyval, base_input, base_time, base_gain, base_conv, base_query,
    base_output, base_head, upscale_input, upscale_time, upscale_gain, upscale_conv,
    upscale_query, upscale_output, upscale_head,
):
    steps = step_ids.reshape(-1)
    level, earlier = alpha_bar(steps), alpha_bar(steps - 50)
    coef = jnp.stack(
        [jnp.sqrt(1.0 - level), lax.rsqrt(level), jnp.sqrt(earlier), jnp.sqrt(1.0 - earlier)], axis=1
    ).reshape(-1)
    code_base = jnp.pad(time_code(step_ids[0], 256), ((0, 6), (0, 0)))
    code_up = jnp.pad(time_code(steps[2:], 64), ((0, 4), (0, 0)))

    remote_params = dict(has_side_effects=True)
    got = pl.pallas_call(
        gather_kernel,
        out_shape=jax.ShapeDtypeStruct((LANE + 2, 2, 3, 16, 32), BF16),
        in_specs=[ANY],
        out_specs=ANY,
        scratch_shapes=[
            pltpu.SemaphoreType.DMA((LANE,)),
            pltpu.SemaphoreType.DMA((LANE + 2,)),
            pltpu.SemaphoreType.DMA((LANE,)),
            pltpu.SemaphoreType.DMA,
        ],
        compiler_params=pltpu.CompilerParams(collective_id=0, **remote_params),
        name="noise_in",
    )(final_noise)

    early, parts = pl.pallas_call(
        work_kernel,
        out_shape=(
            jax.ShapeDtypeStruct((2, 2, 8, 256), F32),
            jax.ShapeDtypeStruct((LANE, 2, 2, 3, 16, 32), BF16),
        ),
        in_specs=[SMEM] + [VMEM] * 12 + [ANY] * 12,
        out_specs=(VMEM, VMEM),
        scratch_shapes=[
            pltpu.VMEM((256, 4096), BF16),
            pltpu.VMEM((6, 4096, 256), BF16),
            pltpu.VMEM((512, 512), BF16),
            pltpu.VMEM((9, 512, 512), BF16),
            pltpu.VMEM((512, 512), BF16),
            pltpu.VMEM((512, 512), BF16),
            pltpu.VMEM((2, 128, 128), BF16),
            pltpu.VMEM((2, 9, 128, 128), BF16),
            pltpu.VMEM((2, 128, 128), BF16),
            pltpu.VMEM((2, 128, 128), BF16),
            pltpu.VMEM((LANE + 2, 2, 3, 16, 32), BF16),
            pltpu.VMEM((256, 4096), BF16),
            pltpu.VMEM((256, 1536), BF16),
            pltpu.VMEM((9, 640, 512), BF16),
            pltpu.VMEM((640, 512), F32),
            pltpu.VMEM((640, 512), BF16),
            pltpu.VMEM((640, 512), BF16),
            pltpu.VMEM((2, 8, 1024), F32),
            pltpu.VMEM((2, 8, 1024), F32),
            pltpu.VMEM((8, 128), F32),
            pltpu.VMEM((8, 128), F32),
            pltpu.VMEM((6, 128, 128), F32),
            pltpu.VMEM((2, 128, 128), BF16),
            pltpu.VMEM((2, 128, 128), BF16),
            pltpu.VMEM((2, 8, 128), BF16),
            pltpu.VMEM((2, 128, 1152), BF16),
            pltpu.VMEM((4, 256, 128), BF16),
            pltpu.VMEM((4, 144, 256), BF16),
            pltpu.VMEM((2, 1, 256), F32),
            pltpu.VMEM((2, 128, 128), F32),
            pltpu.VMEM((8, 512), F32),
            pltpu.VMEM((2, 272, 128), F32),
            pltpu.VMEM((34, 128, 128), F32),
            pltpu.VMEM((34, 384, 128), BF16),
            pltpu.VMEM((2, 2, 256, 128), F32),
            pltpu.SemaphoreType.DMA((16,)),
        ],
        compiler_params=pltpu.CompilerParams(vmem_limit_bytes=56 * 1024 * 1024),
        name="sections",
    )(
        coef, token_ids, base_noise[:, 0], upscale_noise[:, 0], code_base, code_up, t5_gain[None],
        base_input, base_gain, base_head.T, upscale_input, upscale_gain, upscale_head.transpose(0, 2, 1),
        text_states.reshape(256, 4096), base_keyval, upscale_keyval, base_time, base_conv, base_query, base_output,
        upscale_time, upscale_conv, upscale_query, upscale_output, got,
    )

    final_states = pl.pallas_call(
        scatter_kernel,
        out_shape=jax.ShapeDtypeStruct((2, 2, LANE, 3, 16, 32), BF16),
        in_specs=[ANY],
        out_specs=ANY,
        scratch_shapes=[
            pltpu.SemaphoreType.DMA((LANE,)),
            pltpu.SemaphoreType.DMA((LANE,)),
            pltpu.SemaphoreType.DMA,
        ],
        compiler_params=pltpu.CompilerParams(collective_id=1, **remote_params),
        name="results_out",
    )(parts)
    early_states = early[:, :, None, 0:3, :].astype(BF16)
    return early_states, final_states


def solution(mesh):
    placed = [P() for _ in range(23)]
    placed[0] = placed[3] = placed[4] = P(None, "space", None, None)
    placed[5] = P(None, None, None, "space", None)
    return jax.shard_map(
        shards,
        mesh=mesh,
        in_specs=tuple(placed),
        out_specs=(
            P(None, None, "space", None, "segment"),
            P(None, None, "segment", None, "space", None),
        ),
        check_vma=False,
    )
```

profile of v0, /device:TPU:25, one launch (start us, length us, event | category | flops | bytes accessed | tf_op | source)
XLA Modules:
  0.0 112.1 jit_solution(3852312122093776035)
XLA Ops:
  0.6 0.8 convert_reduce_fusion
  1.4 0.8 slice_convert_fusion.1
  2.2 0.1 copy.44
  2.3 0.1 convert_element_type.67
  2.4 0.1 fusion.7
  2.5 0.1 fusion.9
  2.6 0.7 fusion.12.eu
  3.3 1.2 %copy.52 = bf16[2,128,3]{1,2,0:T(4,128)(2,1)} copy(bf16[2,128,3]{1,0,2:T(2,128)(2,1)} %param.45) | data formatting | bytes 3072 | tf_op args[22]
  4.5 1.3 %copy.46.u_in = bf16[2,6,128]{2,1,0:T(8,128)(2,1)} copy(bf16[2,6,128]{2,0,1:T(2,128)(2,1)} %param.39) | data formatting | bytes 6144 | tf_op args[16]
  5.8 1.3 %copy.47.u_gain = f32[2,3,128]{2,1,0:T(4,128)} copy(f32[2,3,128]{2,0,1:T(2,128)} %param.41) | data formatting | bytes 6144 | tf_op args[18]
  7.1 0.8 subtract_sqrt_fusion.1
  7.9 0.1 copy.37
  8.0 0.1 reshape.139
  8.1 0.1 copy.39
  8.2 0.1 reshape.140
  8.3 0.1 copy.40
  8.4 0.1 reshape.143
  8.4 0.1 copy.38
  8.5 0.1 reshape.137
  8.6 0.1 copy.41
  8.7 0.7 reshape.128.coef
  9.4 0.6 fusion.3.eb
  10.0 1.3 %copy_bitcast_fusion = (bf16[2,3,1024]{2,1,0:T(4,128)(2,1)}, bf16[2,3,1024]{2,1,0:T(4,128)(2,1)}) fusion(bf16[2,1,3,1024]{3,0,2,1:T(2,128)(2,1)} %param.27, bf16[2,1,3,1024]{3,0,2,1:T(2,128)(2,1)} %param.26), kind=kLoop, calls=%fused_computation.4 | loop fusion | bytes 49152 | tf_op jit(solution)/shard_map/squeeze | solution.py:571
  11.4 19.4 %noise_in.1.noise_h = bf16[10,2,3,16,32]{4,3,2,1,0:T(8,128)(2,1)} custom-call(bf16[2,32,3,16,32]{4,3,2,1,0:T(8,128)(2,1)} %noise.1), custom_call_target="tpu_custom_call" | custom-call | tf_op jit(solution)/shard_map/noise_in/pallas_call | solution.py:507
  30.7 53.9 %sections.1 = (f32[2,2,8,256]{3,2,1,0:T(8,128)}, bf16[8,2,2,3,16,32]{5,4,3,2,1,0:T(8,128)(2,1)}) custom-call(f32[24]{0:T(128)} %reshape.128.coef, s32[2,32,128]{2,1,0:T(8,128)} %ids.1, bf16[2,3,1024]{2,1,0:T(4,128)(2,1)} %get-tuple-element.19.bx, bf16[2,3,1024]{2,1,0:T(4,128)(2,1)} %get-tuple-element.18.ux, f32[8,512]{1,0:T(8,128)} %fusion.3.eb, ...), custom_call_target="tpu_custom_call" | custom-call | tf_op jit(solution)/shard_map/sections/pallas_call | solution.py:522
  84.7 0.8 fusion.4
  85.4 0.6 copy.48
  86.0 24.3 %results_out.1 = bf16[2,2,8,3,16,32]{5,4,3,2,1,0:T(8,128)(2,1)} custom-call(bf16[8,2,2,3,16,32]{5,4,3,2,1,0:T(8,128)(2,1)} %get-tuple-element.5.parts), custom_call_target="tpu_custom_call" | custom-call | tf_op jit(solution)/shard_map/results_out/pallas_call | solution.py:577
  110.4 1.8 %copy.54 = bf16[2,2,8,3,16,32]{5,4,3,2,1,0:T(8,128)(2,1)} copy(bf16[2,2,8,3,16,32]{5,4,3,2,1,0:T(8,128)(2,1)} %results_out.1) | data formatting | bytes 196608
  (3 shorter events, 0.0 us)
where the time goes:
time: 113 us; the launch traced here: 112 us
  Pallas kernels  97.6 us (86%)
  local copies, waits for them, and re-layouts  9.92 us (9%)
  other arithmetic  3.92 us (3%)
    pallas_call x1, Pallas kernels, shards(): pl.pallas_call(work_kernel, out_shape=(jax.ShapeDtypeStruct((2, 2, 8, 256...  53.9 us
    pallas_call x1, Pallas kernels, shards(): pl.pallas_call(scatter_kernel, out_shape=jax.ShapeDtypeStruct((2, 2, LANE...  24.3 us
    pallas_call x1, Pallas kernels, shards(): pl.pallas_call(gather_kernel, out_shape=jax.ShapeDtypeStruct((LANE + 2, 2...  19.4 us
    unnamed x5, local copies, waits for them, and re-layouts  6.16 us

commit v1 on v0

v1 whole, which is shorter than its diff:
```python
import functools
import math

import jax
import jax.numpy as jnp
from jax import lax
from jax.experimental import pallas as pl
from jax.experimental.pallas import tpu as pltpu
from jax.sharding import PartitionSpec as P

MESH = pl.DeviceIdType.MESH
ANY = pl.BlockSpec(memory_space=pl.ANY)
VMEM = pl.BlockSpec(memory_space=pltpu.VMEM)
SMEM = pl.BlockSpec(memory_space=pltpu.SMEM)
F32, BF16 = jnp.float32, jnp.bfloat16
LOG2E = 1.4426950408889634
SCALE = 0.125 * LOG2E
SEG, LANE = 4, 8

STEPS = 16


def dot(a, b):
    return jnp.dot(a, b, preferred_element_type=F32)


def dot_nt(a, b):
    return lax.dot_general(a, b, (((1,), (1,)), ((), ())), preferred_element_type=F32)


def iota(shape, dim):
    return lax.broadcasted_iota(jnp.int32, shape, dim)


def place():
    z = lax.axis_index("segment")
    p = lax.axis_index("space")
    return z, p // LANE, p % LANE


def remote(src, dst, send, recv, z, p):
    return pltpu.make_async_remote_copy(
        src_ref=src, dst_ref=dst, send_sem=send, recv_sem=recv, device_id=(z, p), device_id_type=MESH
    )


def each_other(z, y, k, body):
    for j in range(LANE):
        @pl.when((y != z) | (k != j))
        def _():
            body(j)


def step_kernel(
    steps, ids, bx, ux, t5g, b_in, b_gain, b_head, u_in, u_gain, u_head,
    noise_h, text_h, bkv_h, ukv_h, btime_h, bconv_h, bq_h, bo_h, utime_h, uconv_h, uq_h, uo_h,
    early, out,
    text_v, kv_w, btime_v, bconv_v, bq_v, bo_v, utime_v, uconv_v, uq_v, uo_v, noise_v,
    ctx, kv, taps, hid, query, att, x8b, x8u, rows8, aug8, gcol, wq_t, wo_t, wh_t, conv_t,
    kcat, vcat, mask_row, mask_col, head8, x2, hid3, act3, c2, early_v,
    snd, snd_b, rcv, snd2, rcv2, sems, send, recv, halo_send, send2, recv2,
):
    z, y, k = place()
    p = y * LANE + k

    barrier = pltpu.get_barrier_semaphore()

    def hello(z_to, p_to):
        pl.semaphore_signal(barrier, inc=1, device_id=(z_to, p_to), device_id_type=MESH)

    each_other(z, y, k, lambda j: hello(y, z * LANE + j))

    @pl.when(z > 0)
    def _():
        hello(y, z * LANE - 1)

    @pl.when(z < SEG - 1)
    def _():
        hello(y, z * LANE + LANE)

    copies = [
        pltpu.make_async_copy(src, dst, sems.at[n])
        for n, (src, dst) in enumerate(
            [
                (noise_h.at[:, pl.ds(z * LANE, LANE)], noise_v),
                (utime_h, utime_v), (uq_h, uq_v), (uo_h, uo_v), (uconv_h, uconv_v), (btime_h, btime_v),
                (text_h, text_v), (bconv_h, bconv_v),
            ]
            + [(bkv_h.at[:, 512 * n : 512 * n + 512], kv_w.at[n]) for n in range(2)]
            + [(ukv_h.at[n], kv_w.at[2, :, 256 * n : 256 * n + 256]) for n in range(2)]
            + [(bq_h, bq_v), (bo_h, bo_v)]
        )
    ]
    for copy in copies:
        copy.start()
    at = dict(noise=0, utime=1, uq=2, uo=3, uconv=4, btime=5, text=6, bconv=7, kv=8, bq=12, bo=13)

    copies[at["noise"]].wait()
    packed = jnp.zeros((LANE * 24, 128), F32)
    for m in range(2):
        rows = noise_v[m].astype(F32)
        for half in range(2):
            group = 2 * m + half
            place_at = (iota((32, 128), 0) + 32 * group == iota((32, 128), 1)).astype(F32).astype(BF16)
            packed += dot(rows[:, :, 8 * half : 8 * half + 8, :].reshape(LANE * 24, 32).astype(BF16), place_at)
    snd[:, 0:24, :] = packed.reshape(LANE, 24, 128)
    snd[:, 24:32, :] = jnp.zeros((LANE, 8, 128), F32)
    snd_b[...] = snd[...].astype(BF16)

    lower = (k == LANE - 1) & (y < SEG - 1)
    upper = (k == 0) & (y > 0)
    extra = jnp.where(lower | upper, LANE, 0)
    pl.semaphore_wait(barrier, LANE - 1 + jnp.where(y != z, 1, 0) + extra)

    def noise_to(j, slot):
        return remote(snd_b.at[j], rcv.at[slot], send.at[j], recv.at[slot], y, z * LANE + j)

    def halo_to(j, slot, to):
        return remote(snd_b.at[j], rcv.at[slot], halo_send.at[j], recv.at[slot], to, z * LANE + j)

    each_other(z, y, k, lambda j: noise_to(j, k).start())
    for cond, slot, step in ((lower, LANE, 1), (upper, LANE + 1, -1)):
        @pl.when(cond)
        def _():
            for j in range(LANE):
                halo_to(j, slot, y + step).start()

    @pl.when(y == z)
    def _():
        rcv[k] = snd_b[k]

    lane128 = iota((128, 128), 1)
    sub128 = iota((128, 128), 0)
    for m in range(2):
        x8b[m] = jnp.zeros((8, 1024), F32)
        x8u[m] = jnp.zeros((8, 1024), F32)
        for c in range(3):
            x8b[m, c : c + 1, :] = bx[c].astype(F32)[m : m + 1]
            x8u[m, c : c + 1, :] = ux[c].astype(F32)[m : m + 1]
        row = jnp.where(ids[m, pl.ds(p, 1), :] != 0, 0.0, -1e30)
        mask_row[m, :, 0:128] = row
        mask_row[m, :, 128:256] = row
        rows8[...] = jnp.broadcast_to(row, (8, 128))
        column = jnp.transpose(rows8[...])[:, 0:1]
        mask_col[m] = jnp.broadcast_to(column, (128, 128))
    head8[...] = jnp.zeros_like(head8)
    head8[0:3, :] = b_head[...].astype(F32)

    def code(width, first):
        row, lane = iota((8, width), 0), iota((8, width), 1)
        step = jnp.zeros((8, width), F32)
        for s in range(2):
            for m in range(2):
                section = min(first + s, 2)
                step = jnp.where(row == 2 * s + m, steps[m, section].astype(F32), step)
        half = width // 2
        angle = step * jnp.exp((-math.log(10000.0) / half) * (lane % half).astype(F32))
        return jnp.where(lane < half, jnp.sin(angle), jnp.cos(angle)).astype(BF16)

    def coefs(s, m):
        step = jnp.full((8, 128), steps[m, s].astype(F32))

        def alpha(at_step):
            return jnp.cos((at_step / 1000.0 + 0.008) * (math.pi / 2 / 1.008)) ** 2

        level, earlier = alpha(step), alpha(step - 50.0)
        return jnp.sqrt(1.0 - level), 1.0 / jnp.sqrt(level), jnp.sqrt(earlier), jnp.sqrt(1.0 - earlier)

    for n in range(1, 5):
        copies[n].wait()
    code_up = code(128, 1)
    code_base = code(512, 0)
    for s in range(2):
        emb = dot(code_up, utime_v[s])
        for m in range(2):
            for c in range(6):
                aug8[c : c + 1, :] = u_in[c].astype(F32)[s : s + 1]
            one = emb[2 * s + m : 2 * s + m + 1, :]
            high = one.astype(BF16).astype(F32)
            aug8[6:7, :] = high
            aug8[7:8, :] = one - high
            x8 = jnp.transpose(aug8[...]).astype(BF16)
            gcol[2 + 2 * s + m, :, 0:8] = x8.astype(F32)
        rows8[...] = jnp.zeros((8, 128), F32)
        for c in range(3):
            rows8[c : c + 1, :] = u_gain[c, s : s + 1, :]
        turned = jnp.transpose(rows8[...])
        gcol[s] = jnp.broadcast_to(turned[:, 0:1] * 0.5, (128, 128))
        wq_t[s] = jnp.transpose(uq_v[s].astype(F32) * (turned[:, 1:2] * SCALE)).astype(BF16)
        wo_t[s] = jnp.transpose(uo_v[s].astype(F32)).astype(BF16)
        rows8[...] = jnp.zeros((8, 128), F32)
        for c in range(3):
            rows8[c : c + 1, :] = u_head[c].astype(F32)[s : s + 1] * u_gain[2, s : s + 1, :]
        wh_t[s] = rows8[...].astype(BF16)
        for tap in range(9):
            conv_t[s, :, 128 * tap : 128 * tap + 128] = jnp.transpose(uconv_v[s, tap].astype(F32)).astype(BF16)

    copies[at["btime"]].wait()
    emb_b = dot(code_base, btime_v[...])
    w_in = b_in[...]
    for m in range(2):
        rolled = pltpu.roll(x8b[m], jnp.mod(32 - 256 * z, 1024), 1)
        own_t = jnp.transpose(rolled[:, 0:384])[0:320, :]
        blk_t = jnp.transpose(x8b[m, :, 0:384])[0:288, :].reshape(9, 32, 8)[:, 0:16, :].reshape(144, 8)
        pix = jnp.concatenate([own_t, blk_t], axis=0)[:, 0:3].astype(BF16)
        hidden = dot(pix, w_in) + emb_b[m : m + 1, :]
        scale = lax.rsqrt(jnp.mean(hidden * hidden, axis=-1, keepdims=True) + 1e-6)
        half = hidden * scale * (b_gain[0:1, :] * 0.5)
        active = half + half * jnp.tanh(half)
        hid[256 * m : 256 * m + 256, :] = hidden[32:288]
        hid[512 + 64 * m : 576 + 64 * m, :] = hidden[320:464].reshape(9, 16, 512)[0:8, 0:8].reshape(64, 512)
        own = active[0:320]
        line = iota((320, 1), 0)
        gone = ((line < 32) & (z == 0)) | ((line >= 288) & (z == SEG - 1))
        own = jnp.where(gone, 0.0, own)
        blk = active[320:464]
        col = line % 32
        bcol = iota((144, 1), 0) % 16
        for b in range(3):
            if b == 0:
                mine = jnp.where(col == 0, 0.0, pltpu.roll(own, 1, 0))
                near = jnp.where(bcol == 0, 0.0, pltpu.roll(blk, 1, 0))
            elif b == 1:
                mine, near = own, blk
            else:
                mine = jnp.where(col == 31, 0.0, pltpu.roll(own, 319, 0))
                near = pltpu.roll(blk, 143, 0)
            mine = mine.astype(BF16)
            near = near.reshape(9, 16, 512)[:, 0:8].reshape(72, 512)
            near = jnp.concatenate([jnp.zeros((8, 512), F32), near], axis=0)
            for a in range(3):
                taps[a, 256 * m : 256 * m + 256, 512 * b : 512 * b + 512] = mine[32 * a : 32 * a + 256]
                taps[a, 512 + 64 * m : 576 + 64 * m, 512 * b : 512 * b + 512] = near[8 * a : 8 * a + 64].astype(BF16)

    copies[at["text"]].wait()

    def norm_step(i, carry):
        at_row = pl.multiple_of(i * 64, 64)
        states = text_v[pl.ds(at_row, 64), :].astype(F32)
        scale = lax.rsqrt(jnp.mean(states * states, axis=-1, keepdims=True) + 1e-6)
        ctx[pl.ds(at_row, 64), :] = (states * scale * t5g[...]).astype(BF16)
        return carry

    lax.fori_loop(0, 4, norm_step, 0)
    copies[at["bconv"]].wait()

    def conv_step(tap, carry):
        hid[...] += dot(taps[tap], bconv_v[tap])
        return carry

    lax.fori_loop(0, 3, conv_step, 0)

    for n in range(3):
        copies[at["kv"] + n].wait()
        if n == 2:
            copies[at["kv"] + 3].wait()
        kv[:, 512 * n : 512 * n + 512] = dot(ctx[...], kv_w[n]).astype(BF16)

    for s in range(2):
        for m in range(2):
            key = kv[128 * m : 128 * m + 128, 1024 + 256 * s : 1152 + 256 * s]
            val = jnp.transpose(kv[128 * m : 128 * m + 128, 1152 + 256 * s : 1280 + 256 * s].astype(F32)).astype(BF16)
            zero = jnp.zeros_like(key)
            kcat[2 * s + m, 0:128, :] = jnp.where(lane128 < 64, key, zero)
            kcat[2 * s + m, 128:256, :] = jnp.where(lane128 < 64, zero, key)
            vcat[2 * s + m, 0:128, 0:128] = jnp.where(sub128 < 64, val, zero)
            vcat[2 * s + m, 0:128, 128:256] = jnp.where(sub128 < 64, zero, val)
            head_of = iota((16, 256), 1) // 128
            vcat[2 * s + m, 128:144, :] = (head_of == iota((16, 256), 0)).astype(F32).astype(BF16)

    copies[at["bq"]].wait()
    copies[at["bo"]].wait()
    h2 = hid[...]
    scale = lax.rsqrt(jnp.mean(h2 * h2, axis=-1, keepdims=True) + 1e-6)
    query[...] = (dot((h2 * scale * b_gain[1:2, :]).astype(BF16), bq_v[...]) * SCALE).astype(BF16)
    for m in range(2):
        for pair in range(4):
            lo = 128 * pair
            key = kv[128 * m : 128 * m + 128, lo : lo + 128]
            val = kv[128 * m : 128 * m + 128, 512 + lo : 640 + lo]
            zero = jnp.zeros_like(key)
            keys = jnp.concatenate([jnp.where(lane128 < 64, key, zero), jnp.where(lane128 < 64, zero, key)], axis=0)
            vals = jnp.concatenate([jnp.where(lane128 < 64, val, zero), jnp.where(lane128 < 64, zero, val)], axis=0)
            ones = ((iota((256, 128), 0) < 128) == (iota((256, 128), 1) < 64)).astype(F32).astype(BF16)
            vals = jnp.concatenate([vals, ones], axis=1)
            q = jnp.concatenate(
                [query[256 * m : 256 * m + 256, lo : lo + 128], query[512 + 64 * m : 576 + 64 * m, lo : lo + 128]], axis=0
            )
            score = dot_nt(q, keys) + mask_row[m]
            left, right = score[:, 0:128], score[:, 128:256]
            left = jnp.exp2(left - jnp.max(left, axis=-1, keepdims=True))
            right = jnp.exp2(right - jnp.max(right, axis=-1, keepdims=True))
            mixed = dot(jnp.concatenate([left, right], axis=1).astype(BF16), vals)
            mixed = (mixed[:, 0:128] / mixed[:, 128:256]).astype(BF16)
            att[256 * m : 256 * m + 256, lo : lo + 128] = mixed[0:256]
            att[512 + 64 * m : 576 + 64 * m, lo : lo + 128] = mixed[256:320]
    h3 = hid[...] + dot(att[...], bo_v[...])
    scale = lax.rsqrt(jnp.mean(h3 * h3, axis=-1, keepdims=True) + 1e-6)
    eps = dot_nt(head8[...].astype(BF16), (h3 * scale * b_gain[2:3, :]).astype(BF16))

    def step_of(noisy, eps, c0, c1, c2_, c3):
        c0, c1, c2_, c3 = (jnp.concatenate([c] * (eps.shape[1] // 128), axis=1) for c in (c0, c1, c2_, c3))
        clean = jnp.clip((noisy - c0 * eps) * c1, -1.0, 1.0)
        return clean, c2_ * clean + c3 * eps

    pick_k, pick_l = iota((256, 128), 0), iota((256, 128), 1)
    noisy = jnp.zeros((8, 128), F32)
    for m in range(2):
        whole = pltpu.roll(x8b[m], jnp.mod(0 - 256 * z, 1024), 1)[:, 0:256]
        _, prior = step_of(whole, eps[:, 256 * m : 256 * m + 256], *coefs(0, m))
        for c in range(3):
            early_v[0, c, m : m + 1, :] = prior[c : c + 1]
        spot = pick_l - 64 * m
        sel = (spot >= 0) & (spot < 64) & (pick_k // 32 == spot // 8) & (pick_k % 32 == spot % 8)
        noisy += dot(x8b[m, :, 0:256].astype(BF16), sel.astype(F32).astype(BF16))
    first_half = iota((8, 128), 1) < 64
    mixed_coefs = tuple(jnp.where(first_half, a, b) for a, b in zip(coefs(0, 0), coefs(0, 1)))
    region, _ = step_of(noisy, eps[:, 512:640], *mixed_coefs)
    region = region.astype(BF16)

    def back(s, m, h2, width):
        sm = 2 * s + m
        scale = lax.rsqrt(jnp.sum(h2 * h2, axis=0, keepdims=True) * (1.0 / 128.0) + 1e-6)
        q = (dot(wq_t[s], h2.astype(BF16)) * scale).astype(BF16)
        score = dot(kcat[sm], q)
        mask = jnp.concatenate([mask_col[m]] * (width // 128), axis=1)
        left, right = score[0:128] + mask, score[128:256] + mask
        left = jnp.exp2(left - jnp.max(left, axis=0, keepdims=True)).astype(BF16)
        right = jnp.exp2(right - jnp.max(right, axis=0, keepdims=True)).astype(BF16)
        mixed = dot(vcat[sm], jnp.concatenate([left, right], axis=0))
        top = mixed[0:64] * (1.0 / mixed[128:129])
        bottom = mixed[64:128] * (1.0 / mixed[129:130])
        h3 = h2 + dot(wo_t[s], jnp.concatenate([top, bottom], axis=0).astype(BF16))
        scale = lax.rsqrt(jnp.sum(h3 * h3, axis=0, keepdims=True) * (1.0 / 128.0) + 1e-6)
        return dot(wh_t[s], h3.astype(BF16)) * scale

    def activate(hidden, s, width):
        scale = lax.rsqrt(jnp.sum(hidden * hidden, axis=0, keepdims=True) * (1.0 / 128.0) + 1e-6)
        gain = jnp.concatenate([gcol[s]] * (width // 128), axis=1)
        half = hidden * scale * gain
        return half + half * jnp.tanh(half)

    lanes = iota((1, 384), 1)
    row_of = 8 * z - 2 + lanes // 32
    col_of = lanes % 32
    inside = (row_of >= 0) & (row_of < 32)
    spread_k = iota((128, 384), 0)
    spread_l = iota((128, 384), 1)
    spread_at = ((8 * z - 2 + spread_l // 32 + 4) // 4 - 1) * 8 + (spread_l % 32) // 4
    for m in range(2):
        x = pltpu.roll(x8u[m], jnp.mod(64 - 256 * z, 1024), 1)[:, 0:384]
        sel = (spread_k == spread_at + 64 * m) & (spread_at >= 0) & (spread_at < 64)
        cond = dot(region, sel.astype(F32).astype(BF16))
        which = iota((8, 384), 0)
        cond = pltpu.roll(cond, 3, 0)
        x8 = jnp.where(which < 3, x, jnp.where(which < 6, cond, 1.0))
        hidden = dot(gcol[2 + m, :, 0:8].astype(BF16), x8.astype(BF16))
        active = jnp.where(inside, activate(hidden, 0, 384), 0.0)
        stack = [
            jnp.where(col_of == 0, 0.0, pltpu.roll(active, 1, 1)),
            active,
            jnp.where(col_of == 31, 0.0, pltpu.roll(active, 383, 1)),
        ]
        stack = [pltpu.roll(one, 32, 1) for one in stack] + stack + [pltpu.roll(one, 352, 1) for one in stack]
        stack = jnp.concatenate([one.astype(BF16) for one in stack], axis=0)
        h2 = hidden + dot(conv_t[0], stack)
        eps = back(0, m, h2, 384)
        clean, prior = step_of(x, eps, *coefs(1, m))
        prior = pltpu.roll(prior, 320, 1)[:, 0:256]
        for c in range(3):
            early_v[1, c, m : m + 1, :] = prior[c : c + 1]
        clean = clean.astype(BF16)
        pick_k, pick_l = iota((384, 128), 0), iota((384, 128), 1)

        def rows_at(first):
            sel = (pick_k // 32 == first + 2 * (pick_l // 32)) & (pick_k % 32 == pick_l % 32)
            return dot(clean, sel.astype(F32).astype(BF16))

        x2[m] = jnp.ones((34 * 8, 128), F32)
        even, odd = rows_at(2), rows_at(3)
        above, below = rows_at(1), rows_at(4)
        for c in range(3):
            x2[m, pl.ds(8 + 3 + c, 16, 8), :] = jnp.broadcast_to(even[c : c + 1], (16, 128))
            x2[m, pl.ds(8 * 17 + 3 + c, 16, 8), :] = jnp.broadcast_to(odd[c : c + 1], (16, 128))
            x2[m, 3 + c : 4 + c, :] = above[c : c + 1]
            x2[m, 33 * 8 + 3 + c : 33 * 8 + 4 + c, :] = below[c : c + 1]

    pass

    early[...] = early_v[...].astype(BF16)
    each_other(z, y, k, lambda j: noise_to(j, j).wait_recv())

    @pl.when(z > 0)
    def _():
        noise_to(0, LANE).wait_recv()

    @pl.when(z < SEG - 1)
    def _():
        noise_to(0, LANE + 1).wait_recv()

    @pl.when(z == 0)
    def _():
        rcv[LANE] = jnp.zeros((32, 128), BF16)

    @pl.when(z == SEG - 1)
    def _():
        rcv[LANE + 1] = jnp.zeros((32, 128), BF16)

    lane1 = iota((1, 128), 1)

    def regroup(value, source, target):
        by = 32 * (target - source) % 128
        return pltpu.roll(value, by, 1) if by else value

    blocks = [rcv[n].astype(F32)[0:24] for n in range(LANE + 2)]
    for m in range(2):
        edge = {}
        for h in range(2):
            for half in range(2):
                group = 2 * m + half
                total = regroup(blocks[h], group, 0)
                for g in range(1, 4):
                    total = jnp.where(lane1 // 32 == g, regroup(blocks[2 * g + h], group, g), total)
                edge[h, half] = total
                for c in range(3):
                    x2[m, pl.ds(8 * (1 + 16 * h + 8 * half) + c, 8, 8), :] = total[8 * c : 8 * c + 8]
        top = regroup(blocks[LANE], 2 * m + 1, 0)
        low = regroup(blocks[LANE + 1], 2 * m, 3)
        over = pltpu.roll(edge[1, 1], 32, 1)
        under = pltpu.roll(edge[0, 0], 96, 1)
        for c in range(3):
            x2[m, c : c + 1, :] = jnp.where(lane1 < 32, top, over)[8 * c + 7 : 8 * c + 8]
            x2[m, 33 * 8 + c : 33 * 8 + c + 1, :] = jnp.where(lane1 >= 96, low, under)[8 * c : 8 * c + 1]

    lane2 = iota((1, 256), 1) % 128
    col2 = lane2 % 32
    for m in range(2):
        FT = 17
        colf = iota((1, 128 * FT), 1) % 32
        for n in range(34 // FT):
            t = n * FT
            rows = x2[m, t * 8 : (t + FT) * 8, :]
            x8 = jnp.concatenate([rows[8 * e : 8 * e + 8] for e in range(FT)], axis=1).astype(BF16)
            hidden = dot(gcol[4 + m, :, 0:8].astype(BF16), x8)
            active = activate(hidden, 1, 128 * FT)
            tile = t + iota((1, 128 * FT), 1) // 128
            lanef = iota((1, 128 * FT), 1) % 128
            gone = ((tile == 0) & (lanef < 32) & (z == 0)) | ((tile == 33) & (lanef >= 96) & (z == SEG - 1))
            active = jnp.where(gone, 0.0, active)
            for h in range(FT):
                one = active[:, 128 * h : 128 * h + 128]
                hid3[t + h] = hidden[:, 128 * h : 128 * h + 128]
                act3[t + h, 0:128] = jnp.where(col2[:, 0:128] == 0, 0.0, pltpu.roll(one, 1, 1)).astype(BF16)
                act3[t + h, 128:256] = one.astype(BF16)
                act3[t + h, 256:384] = jnp.where(col2[:, 0:128] == 31, 0.0, pltpu.roll(one, 127, 1)).astype(BF16)

        def back_step(n, carry):
            i = n * STEPS
            tiles = [act3[i + e] for e in range(STEPS + 2)]
            stack = jnp.concatenate(
                [jnp.concatenate(tiles[a : a + STEPS], axis=1) for a in range(3)], axis=0
            )
            h2 = jnp.concatenate([hid3[i + 1 + e] for e in range(STEPS)], axis=1) + dot(conv_t[1], stack)
            eps = back(1, m, h2, 128 * STEPS)
            rows = x2[m, pl.ds(pl.multiple_of((i + 1) * 8, 8), 8 * STEPS), :]
            noisy = jnp.concatenate([rows[8 * e : 8 * e + 8] for e in range(STEPS)], axis=1)
            clean, prior = step_of(noisy, eps, *coefs(2, m))
            for e in range(STEPS):
                spot_at = pl.ds(pl.multiple_of((i + e) * 8, 8), 8)
                c2[0, m, spot_at, :] = clean[:, 128 * e : 128 * e + 128]
                c2[1, m, spot_at, :] = prior[:, 128 * e : 128 * e + 128]
            return carry

        lax.fori_loop(0, 32 // STEPS, back_step, 0)

    def result_to(j, slot):
        return remote(snd2.at[j], rcv2.at[slot], send2.at[j], recv2.at[slot], y, z * LANE + j)

    for j in range(LANE):
        rows = []
        for c in range(3):
            total = None
            for o in range(2):
                for m in range(2):
                    one = regroup(c2[o, m, pl.ds(128 * (j % 2) + c, 16, 8), :], j // 2, 2 * o + m)
                    total = one if total is None else jnp.where(lane1 // 32 == 2 * o + m, one, total)
            rows.append(total)
        snd2[j] = jnp.concatenate(rows, axis=0).astype(BF16)

        @pl.when((y != z) | (k != j))
        def _():
            result_to(j, k).start()

    @pl.when(y == z)
    def _():
        rcv2[k] = snd2[k]

    each_other(z, y, k, lambda j: noise_to(j, k).wait_send())
    for cond, slot, step in ((lower, LANE, 1), (upper, LANE + 1, -1)):
        @pl.when(cond)
        def _():
            for j in range(LANE):
                halo_to(j, slot, y + step).wait_send()

    each_other(z, y, k, lambda j: result_to(j, j).wait_recv())
    for j in range(LANE):
        whole = rcv2[j].astype(F32)
        for o in range(2):
            for m in range(2):
                one = regroup(whole, 2 * o + m, 0)[:, 0:32].astype(BF16)
                for c in range(3):
                    out[o, m, j, c] = one[16 * c : 16 * c + 16]
    each_other(z, y, k, lambda j: result_to(j, k).wait_send())


def shards(
    text_states, token_ids, step_ids, base_noise, upscale_noise, final_noise, t5_gain,
    base_keyval, upscale_keyval, base_input, base_time, base_gain, base_conv, base_query,
    base_output, base_head, upscale_input, upscale_time, upscale_gain, upscale_conv,
    upscale_query, upscale_output, upscale_head,
):
    early, final_states = pl.pallas_call(
        step_kernel,
        out_shape=(
            jax.ShapeDtypeStruct((2, 3, 2, 256), BF16),
            jax.ShapeDtypeStruct((2, 2, LANE, 3, 16, 32), BF16),
        ),
        in_specs=[SMEM] + [VMEM] * 10 + [ANY] * 12,
        out_specs=(VMEM, VMEM),
        scratch_shapes=[
            pltpu.VMEM((256, 4096), BF16),
            pltpu.VMEM((3, 4096, 512), BF16),
            pltpu.VMEM((512, 512), BF16),
            pltpu.VMEM((3, 1536, 512), BF16),
            pltpu.VMEM((512, 512), BF16),
            pltpu.VMEM((512, 512), BF16),
            pltpu.VMEM((2, 128, 128), BF16),
            pltpu.VMEM((2, 9, 128, 128), BF16),
            pltpu.VMEM((2, 128, 128), BF16),
            pltpu.VMEM((2, 128, 128), BF16),
            pltpu.VMEM((2, LANE, 3, 16, 32), BF16),
            pltpu.VMEM((256, 4096), BF16),
            pltpu.VMEM((256, 1536), BF16),
            pltpu.VMEM((3, 640, 1536), BF16),
            pltpu.VMEM((640, 512), F32),
            pltpu.VMEM((640, 512), BF16),
            pltpu.VMEM((640, 512), BF16),
            pltpu.VMEM((2, 8, 1024), F32),
            pltpu.VMEM((2, 8, 1024), F32),
            pltpu.VMEM((8, 128), F32),
            pltpu.VMEM((8, 128), F32),
            pltpu.VMEM((6, 128, 128), F32),
            pltpu.VMEM((2, 128, 128), BF16),
            pltpu.VMEM((2, 128, 128), BF16),
            pltpu.VMEM((2, 8, 128), BF16),
            pltpu.VMEM((2, 128, 1152), BF16),
            pltpu.VMEM((4, 256, 128), BF16),
            pltpu.VMEM((4, 144, 256), BF16),
            pltpu.VMEM((2, 1, 256), F32),
            pltpu.VMEM((2, 128, 128), F32),
            pltpu.VMEM((8, 512), F32),
            pltpu.VMEM((2, 272, 128), F32),
            pltpu.VMEM((34, 128, 128), F32),
            pltpu.VMEM((34, 384, 128), BF16),
            pltpu.VMEM((2, 2, 256, 128), F32),
            pltpu.VMEM((2, 3, 2, 256), F32),
            pltpu.VMEM((LANE, 32, 128), F32),
            pltpu.VMEM((LANE, 32, 128), BF16),
            pltpu.VMEM((LANE + 2, 32, 128), BF16),
            pltpu.VMEM((LANE, 48, 128), BF16),
            pltpu.VMEM((LANE, 48, 128), BF16),
            pltpu.SemaphoreType.DMA((14,)),
            pltpu.SemaphoreType.DMA((LANE,)),
            pltpu.SemaphoreType.DMA((LANE + 2,)),
            pltpu.SemaphoreType.DMA((LANE,)),
            pltpu.SemaphoreType.DMA((LANE,)),
            pltpu.SemaphoreType.DMA((LANE,)),
        ],
        compiler_params=pltpu.CompilerParams(
            vmem_limit_bytes=56 * 1024 * 1024, collective_id=0, has_side_effects=True
        ),
        name="denoise",
    )(
        step_ids.T, token_ids, base_noise[:, 0].transpose(1, 0, 2), upscale_noise[:, 0].transpose(1, 0, 2), t5_gain[None],
        base_input, base_gain, base_head.T, upscale_input.transpose(1, 0, 2), upscale_gain.transpose(1, 0, 2),
        upscale_head.transpose(2, 0, 1), final_noise,
        text_states.reshape(256, 4096), base_keyval, upscale_keyval, base_time, base_conv.reshape(3, 1536, 512),
        base_query, base_output, upscale_time, upscale_conv, upscale_query, upscale_output,
    )
    return early.transpose(0, 2, 1, 3)[:, :, None], final_states


def solution(mesh):
    placed = [P() for _ in range(23)]
    placed[0] = placed[3] = placed[4] = P(None, "space", None, None)
    placed[5] = P(None, None, None, "space", None)
    return jax.shard_map(
        shards,
        mesh=mesh,
        in_specs=tuple(placed),
        out_specs=(
            P(None, None, "space", None, "segment"),
            P(None, None, "segment", None, "space", None),
        ),
        check_vma=False,
    )
```

time: 113 us -> 47.6 us (0.42)
  the two profiles are of different devices: /device:TPU:25 before, /device:TPU:17 now
where the time goes in v1:
time: 47.6 us; the launch traced here: 47.4 us
  Pallas kernels  43.6 us (92%)
  local copies, waits for them, and re-layouts  3.06 us (6%)
  between operations  0.65 us (1%)
    pallas_call x1, Pallas kernels, shards(): pl.pallas_call(step_kernel, out_shape=(jax.ShapeDtypeStruct((2, 3, 2, 256...  43.6 us
    unnamed x2, local copies, waits for them, and re-layouts  3.06 us

profile of v1, /device:TPU:17, one launch (start us, length us, event | category | flops | bytes accessed | tf_op | source)
XLA Modules:
  0.0 47.4 jit_solution(15240444275856538709)
XLA Ops:
  0.6 43.6 %denoise.1 = (bf16[2,3,2,256]{3,2,1,0:T(2,128)(2,1)}, bf16[2,2,8,3,16,32]{5,4,3,2,1,0:T(8,128)(2,1)}) custom-call(s32[2,3]{1,0:T(2,128)} %bitcast.29, s32[2,32,128]{2,1,0:T(8,128)} %ids.1, bf16[3,2,1024]{2,1,0:T(2,128)(2,1)} %bitcast.22, bf16[3,2,1024]{2,1,0:T(2,128)(2,1)} %bitcast.23, f32[1,4096]{1,0:T(1,128)} %bitcast.21, bf16[3,512]{1,0:T(4,128)(2,1)} %b_in.1, ...), custom_call_target="tpu_custom_call" | custom-call | tf_op jit(solution)/shard_map/denoise/pallas_call | solution.py:522
  44.3 1.3 %copy.28 = bf16[2,2,1,3,256]{4,1,3,2,0:T(2,128)(2,1)} copy(bf16[2,2,1,3,256]{4,1,3,2,0:T(2,128)(2,1)} %bitcast.24) | data formatting | bytes 12288
  45.6 1.8 %copy.29 = bf16[2,2,8,3,16,32]{5,4,3,2,1,0:T(8,128)(2,1)} copy(bf16[2,2,8,3,16,32]{5,4,3,2,1,0:T(8,128)(2,1)} %get-tuple-element.11) | data formatting | bytes 196608

commit v2 on v1

--- a/solution.py
+++ b/solution.py
@@ -17,7 +17,7 @@
 SCALE = 0.125 * LOG2E
 SEG, LANE = 4, 8
 
-STEPS = 16
+STEPS = 32
 
 
 def dot(a, b):
@@ -54,11 +54,11 @@
 def step_kernel(
     steps, ids, bx, ux, t5g, b_in, b_gain, b_head, u_in, u_gain, u_head,
     noise_h, text_h, bkv_h, ukv_h, btime_h, bconv_h, bq_h, bo_h, utime_h, uconv_h, uq_h, uo_h,
-    early, out,
+    early, rcv2,
     text_v, kv_w, btime_v, bconv_v, bq_v, bo_v, utime_v, uconv_v, uq_v, uo_v, noise_v,
     ctx, kv, taps, hid, query, att, x8b, x8u, rows8, aug8, gcol, wq_t, wo_t, wh_t, conv_t,
     kcat, vcat, mask_row, mask_col, head8, x2, hid3, act3, c2, early_v,
-    snd, snd_b, rcv, snd2, rcv2, sems, send, recv, halo_send, send2, recv2,
+    snd, snd_b, rcv, snd2, sems, send, recv, halo_send, send2, recv2,
 ):
     z, y, k = place()
     p = y * LANE + k
@@ -229,8 +229,8 @@
             near = near.reshape(9, 16, 512)[:, 0:8].reshape(72, 512)
             near = jnp.concatenate([jnp.zeros((8, 512), F32), near], axis=0)
             for a in range(3):
-                taps[a, 256 * m : 256 * m + 256, 512 * b : 512 * b + 512] = mine[32 * a : 32 * a + 256]
-                taps[a, 512 + 64 * m : 576 + 64 * m, 512 * b : 512 * b + 512] = near[8 * a : 8 * a + 64].astype(BF16)
+                taps[256 * m : 256 * m + 256, 512 * (3 * a + b) : 512 * (3 * a + b) + 512] = mine[32 * a : 32 * a + 256]
+                taps[512 + 64 * m : 576 + 64 * m, 512 * (3 * a + b) : 512 * (3 * a + b) + 512] = near[8 * a : 8 * a + 64].astype(BF16)
 
     copies[at["text"]].wait()
 
@@ -244,11 +244,7 @@
     lax.fori_loop(0, 4, norm_step, 0)
     copies[at["bconv"]].wait()
 
-    def conv_step(tap, carry):
-        hid[...] += dot(taps[tap], bconv_v[tap])
-        return carry
-
-    lax.fori_loop(0, 3, conv_step, 0)
+    hid[...] += dot(taps[...], bconv_v[...])
 
     for n in range(3):
         copies[at["kv"] + n].wait()
@@ -311,26 +307,29 @@
         for c in range(3):
             early_v[0, c, m : m + 1, :] = prior[c : c + 1]
         spot = pick_l - 64 * m
-        sel = (spot >= 0) & (spot < 64) & (pick_k // 32 == spot // 8) & (pick_k % 32 == spot % 8)
+        sel = (spot >= 0) & (spot < 64) & ((pick_k >> 5) == (spot >> 3)) & ((pick_k & 31) == (spot & 7))
         noisy += dot(x8b[m, :, 0:256].astype(BF16), sel.astype(F32).astype(BF16))
     first_half = iota((8, 128), 1) < 64
     mixed_coefs = tuple(jnp.where(first_half, a, b) for a, b in zip(coefs(0, 0), coefs(0, 1)))
     region, _ = step_of(noisy, eps[:, 512:640], *mixed_coefs)
     region = region.astype(BF16)
 
-    def back(s, m, h2, width):
-        sm = 2 * s + m
+    def back(s, ms, h2, width):
         scale = lax.rsqrt(jnp.sum(h2 * h2, axis=0, keepdims=True) * (1.0 / 128.0) + 1e-6)
         q = (dot(wq_t[s], h2.astype(BF16)) * scale).astype(BF16)
-        score = dot(kcat[sm], q)
-        mask = jnp.concatenate([mask_col[m]] * (width // 128), axis=1)
-        left, right = score[0:128] + mask, score[128:256] + mask
-        left = jnp.exp2(left - jnp.max(left, axis=0, keepdims=True)).astype(BF16)
-        right = jnp.exp2(right - jnp.max(right, axis=0, keepdims=True)).astype(BF16)
-        mixed = dot(vcat[sm], jnp.concatenate([left, right], axis=0))
-        top = mixed[0:64] * (1.0 / mixed[128:129])
-        bottom = mixed[64:128] * (1.0 / mixed[129:130])
-        h3 = h2 + dot(wo_t[s], jnp.concatenate([top, bottom], axis=0).astype(BF16))
+        both = []
+        for n, m in enumerate(ms):
+            score = dot(kcat[2 * s + m], q[:, width * n : width * n + width])
+            mask = jnp.concatenate([mask_col[m]] * (width // 128), axis=1)
+            left, right = score[0:128] + mask, score[128:256] + mask
+            left = jnp.exp2(left - jnp.max(left, axis=0, keepdims=True)).astype(BF16)
+            right = jnp.exp2(right - jnp.max(right, axis=0, keepdims=True)).astype(BF16)
+            mixed = dot(vcat[2 * s + m], jnp.concatenate([left, right], axis=0))
+            top = mixed[0:64] * (1.0 / mixed[128:129])
+            bottom = mixed[64:128] * (1.0 / mixed[129:130])
+            both.append(jnp.concatenate([top, bottom], axis=0).astype(BF16))
+        both = both[0] if len(both) == 1 else jnp.concatenate(both, axis=1)
+        h3 = h2 + dot(wo_t[s], both)
         scale = lax.rsqrt(jnp.sum(h3 * h3, axis=0, keepdims=True) * (1.0 / 128.0) + 1e-6)
         return dot(wh_t[s], h3.astype(BF16)) * scale
 
@@ -340,41 +339,53 @@
         half = hidden * scale * gain
         return half + half * jnp.tanh(half)
 
-    lanes = iota((1, 384), 1)
-    row_of = 8 * z - 2 + lanes // 32
-    col_of = lanes % 32
+    lane1 = iota((1, 128), 1)
+
+    def regroup(value, source, target):
+        by = 32 * (target - source) % 128
+        return pltpu.roll(value, by, 1) if by else value
+
+    lanes = iota((1, 768), 1)
+    lanes = jnp.where(lanes >= 384, lanes - 384, lanes)
+    row_of = 8 * z - 2 + (lanes >> 5)
+    col_of = lanes & 31
     inside = (row_of >= 0) & (row_of < 32)
     spread_k = iota((128, 384), 0)
     spread_l = iota((128, 384), 1)
-    spread_at = ((8 * z - 2 + spread_l // 32 + 4) // 4 - 1) * 8 + (spread_l % 32) // 4
+    spread_at = (((8 * z + 2 + (spread_l >> 5)) >> 2) - 1) * 8 + ((spread_l & 31) >> 2)
+    spread_at = jnp.where((spread_at >= 0) & (spread_at < 64), spread_at, -1000)
+    which = iota((8, 384), 0)
+    noisy, hidden = [], []
     for m in range(2):
         x = pltpu.roll(x8u[m], jnp.mod(64 - 256 * z, 1024), 1)[:, 0:384]
-        sel = (spread_k == spread_at + 64 * m) & (spread_at >= 0) & (spread_at < 64)
-        cond = dot(region, sel.astype(F32).astype(BF16))
-        which = iota((8, 384), 0)
-        cond = pltpu.roll(cond, 3, 0)
+        cond = pltpu.roll(dot(region, (spread_k == spread_at + 64 * m).astype(F32).astype(BF16)), 3, 0)
         x8 = jnp.where(which < 3, x, jnp.where(which < 6, cond, 1.0))
-        hidden = dot(gcol[2 + m, :, 0:8].astype(BF16), x8.astype(BF16))
-        active = jnp.where(inside, activate(hidden, 0, 384), 0.0)
-        stack = [
-            jnp.where(col_of == 0, 0.0, pltpu.roll(active, 1, 1)),
-            active,
-            jnp.where(col_of == 31, 0.0, pltpu.roll(active, 383, 1)),
-        ]
-        stack = [pltpu.roll(one, 32, 1) for one in stack] + stack + [pltpu.roll(one, 352, 1) for one in stack]
-        stack = jnp.concatenate([one.astype(BF16) for one in stack], axis=0)
-        h2 = hidden + dot(conv_t[0], stack)
-        eps = back(0, m, h2, 384)
-        clean, prior = step_of(x, eps, *coefs(1, m))
+        hidden.append(dot(gcol[2 + m, :, 0:8].astype(BF16), x8.astype(BF16)))
+        noisy.append(x)
+    hidden = jnp.concatenate(hidden, axis=1)
+    active = jnp.where(inside, activate(hidden, 0, 768), 0.0)
+    stack = [
+        jnp.where(col_of == 0, 0.0, pltpu.roll(active, 1, 1)),
+        active,
+        jnp.where(col_of == 31, 0.0, pltpu.roll(active, 767, 1)),
+    ]
+    stack = [pltpu.roll(one, 32, 1) for one in stack] + stack + [pltpu.roll(one, 736, 1) for one in stack]
+    stack = jnp.concatenate([one.astype(BF16) for one in stack], axis=0)
+    eps = back(0, (0, 1), hidden + dot(conv_t[0], stack), 384)
+    for m in range(2):
+        clean, prior = step_of(noisy[m], eps[:, 384 * m : 384 * m + 384], *coefs(1, m))
         prior = pltpu.roll(prior, 320, 1)[:, 0:256]
         for c in range(3):
             early_v[1, c, m : m + 1, :] = prior[c : c + 1]
-        clean = clean.astype(BF16)
-        pick_k, pick_l = iota((384, 128), 0), iota((384, 128), 1)
+        clean = clean.astype(BF16).astype(F32)
 
         def rows_at(first):
-            sel = (pick_k // 32 == first + 2 * (pick_l // 32)) & (pick_k % 32 == pick_l % 32)
-            return dot(clean, sel.astype(F32).astype(BF16))
+            total = None
+            for g in range(4):
+                row = first + 2 * g
+                one = regroup(clean[:, 128 * (row // 4) : 128 * (row // 4) + 128], row % 4, g)
+                total = one if total is None else jnp.where((lane1 >> 5) == g, one, total)
+            return total
 
         x2[m] = jnp.ones((34 * 8, 128), F32)
         even, odd = rows_at(2), rows_at(3)
@@ -385,8 +396,6 @@
             x2[m, 3 + c : 4 + c, :] = above[c : c + 1]
             x2[m, 33 * 8 + 3 + c : 33 * 8 + 4 + c, :] = below[c : c + 1]
 
-    pass
-
     early[...] = early_v[...].astype(BF16)
     each_other(z, y, k, lambda j: noise_to(j, j).wait_recv())
 
@@ -405,12 +414,6 @@
     @pl.when(z == SEG - 1)
     def _():
         rcv[LANE + 1] = jnp.zeros((32, 128), BF16)
-
-    lane1 = iota((1, 128), 1)
-
-    def regroup(value, source, target):
-        by = 32 * (target - source) % 128
-        return pltpu.roll(value, by, 1) if by else value
 
     blocks = [rcv[n].astype(F32)[0:24] for n in range(LANE + 2)]
     for m in range(2):
@@ -420,7 +423,7 @@
                 group = 2 * m + half
                 total = regroup(blocks[h], group, 0)
                 for g in range(1, 4):
-                    total = jnp.where(lane1 // 32 == g, regroup(blocks[2 * g + h], group, g), total)
+                    total = jnp.where((lane1 >> 5) == g, regroup(blocks[2 * g + h], group, g), total)
                 edge[h, half] = total
                 for c in range(3):
                     x2[m, pl.ds(8 * (1 + 16 * h + 8 * half) + c, 8, 8), :] = total[8 * c : 8 * c + 8]
@@ -432,68 +435,62 @@
             x2[m, c : c + 1, :] = jnp.where(lane1 < 32, top, over)[8 * c + 7 : 8 * c + 8]
             x2[m, 33 * 8 + c : 33 * 8 + c + 1, :] = jnp.where(lane1 >= 96, low, under)[8 * c : 8 * c + 1]
 
-    lane2 = iota((1, 256), 1) % 128
-    col2 = lane2 % 32
-    for m in range(2):
-        FT = 17
-        colf = iota((1, 128 * FT), 1) % 32
+    def result_to(m, j, slot):
+        return remote(snd2.at[m, j], rcv2.at[m, slot], send2.at[m, j], recv2.at[m, slot], y, z * LANE + j)
+
+    FT = 17
+    lanef = iota((1, 128 * FT), 1)
+    colf = iota((1, 128), 1) & 31
+    for m in range(2):
         for n in range(34 // FT):
             t = n * FT
             rows = x2[m, t * 8 : (t + FT) * 8, :]
             x8 = jnp.concatenate([rows[8 * e : 8 * e + 8] for e in range(FT)], axis=1).astype(BF16)
             hidden = dot(gcol[4 + m, :, 0:8].astype(BF16), x8)
             active = activate(hidden, 1, 128 * FT)
-            tile = t + iota((1, 128 * FT), 1) // 128
-            lanef = iota((1, 128 * FT), 1) % 128
-            gone = ((tile == 0) & (lanef < 32) & (z == 0)) | ((tile == 33) & (lanef >= 96) & (z == SEG - 1))
-            active = jnp.where(gone, 0.0, active)
+            if n == 0:
+                active = jnp.where((lanef < 32) & (z == 0), 0.0, active)
+            else:
+                active = jnp.where((lanef >= 128 * FT - 32) & (z == SEG - 1), 0.0, active)
             for h in range(FT):
                 one = active[:, 128 * h : 128 * h + 128]
-                hid3[t + h] = hidden[:, 128 * h : 128 * h + 128]
-                act3[t + h, 0:128] = jnp.where(col2[:, 0:128] == 0, 0.0, pltpu.roll(one, 1, 1)).astype(BF16)
-                act3[t + h, 128:256] = one.astype(BF16)
-                act3[t + h, 256:384] = jnp.where(col2[:, 0:128] == 31, 0.0, pltpu.roll(one, 127, 1)).astype(BF16)
-
-        def back_step(n, carry):
-            i = n * STEPS
-            tiles = [act3[i + e] for e in range(STEPS + 2)]
+                hid3[m, t + h] = hidden[:, 128 * h : 128 * h + 128]
+                act3[m, t + h, 0:128] = jnp.where(colf == 0, 0.0, pltpu.roll(one, 1, 1)).astype(BF16)
+                act3[m, t + h, 128:256] = one.astype(BF16)
+                act3[m, t + h, 256:384] = jnp.where(colf == 31, 0.0, pltpu.roll(one, 127, 1)).astype(BF16)
+
+        for i in range(0, 32, STEPS):
+            tiles = [act3[m, i + e] for e in range(STEPS + 2)]
             stack = jnp.concatenate(
                 [jnp.concatenate(tiles[a : a + STEPS], axis=1) for a in range(3)], axis=0
             )
-            h2 = jnp.concatenate([hid3[i + 1 + e] for e in range(STEPS)], axis=1) + dot(conv_t[1], stack)
-            eps = back(1, m, h2, 128 * STEPS)
-            rows = x2[m, pl.ds(pl.multiple_of((i + 1) * 8, 8), 8 * STEPS), :]
+            h2 = jnp.concatenate([hid3[m, i + 1 + e] for e in range(STEPS)], axis=1) + dot(conv_t[1], stack)
+            eps = back(1, (m,), h2, 128 * STEPS)
+            rows = x2[m, (i + 1) * 8 : (i + 1 + STEPS) * 8, :]
             noisy = jnp.concatenate([rows[8 * e : 8 * e + 8] for e in range(STEPS)], axis=1)
             clean, prior = step_of(noisy, eps, *coefs(2, m))
             for e in range(STEPS):
-                spot_at = pl.ds(pl.multiple_of((i + e) * 8, 8), 8)
-                c2[0, m, spot_at, :] = clean[:, 128 * e : 128 * e + 128]
-                c2[1, m, spot_at, :] = prior[:, 128 * e : 128 * e + 128]
-            return carry
-
-        lax.fori_loop(0, 32 // STEPS, back_step, 0)
-
-    def result_to(j, slot):
-        return remote(snd2.at[j], rcv2.at[slot], send2.at[j], recv2.at[slot], y, z * LANE + j)
-
-    for j in range(LANE):
-        rows = []
-        for c in range(3):
-            total = None
-            for o in range(2):
-                for m in range(2):
-                    one = regroup(c2[o, m, pl.ds(128 * (j % 2) + c, 16, 8), :], j // 2, 2 * o + m)
-                    total = one if total is None else jnp.where(lane1 // 32 == 2 * o + m, one, total)
-            rows.append(total)
-        snd2[j] = jnp.concatenate(rows, axis=0).astype(BF16)
-
-        @pl.when((y != z) | (k != j))
+                c2[0, m, (i + e) * 8 : (i + e) * 8 + 8, :] = clean[:, 128 * e : 128 * e + 128]
+                c2[1, m, (i + e) * 8 : (i + e) * 8 + 8, :] = prior[:, 128 * e : 128 * e + 128]
+
+        for j in range(LANE):
+            rows = []
+            for c in range(3):
+                total = None
+                for o in range(2):
+                    for half in range(2):
+                        one = c2[o, m, pl.ds(128 * (j % 2) + 64 * half + c, 8, 8), :]
+                        one = regroup(one, j // 2, 2 * o + half)
+                        total = one if total is None else jnp.where((lane1 >> 5) == 2 * o + half, one, total)
+                rows.append(total)
+            rows.append(jnp.zeros((8, 128), F32))
+            snd2[m, j] = jnp.concatenate(rows, axis=0).astype(BF16)
+
+        each_other(z, y, k, lambda j: result_to(m, j, k).start())
+
+        @pl.when(y == z)
         def _():
-            result_to(j, k).start()
-
-    @pl.when(y == z)
-    def _():
-        rcv2[k] = snd2[k]
+            rcv2[m, k] = snd2[m, k]
 
     each_other(z, y, k, lambda j: noise_to(j, k).wait_send())
     for cond, slot, step in ((lower, LANE, 1), (upper, LANE + 1, -1)):
@@ -502,15 +499,25 @@
             for j in range(LANE):
                 halo_to(j, slot, y + step).wait_send()
 
-    each_other(z, y, k, lambda j: result_to(j, j).wait_recv())
-    for j in range(LANE):
-        whole = rcv2[j].astype(F32)
-        for o in range(2):
-            for m in range(2):
-                one = regroup(whole, 2 * o + m, 0)[:, 0:32].astype(BF16)
+    for m in range(2):
+        each_other(z, y, k, lambda j: result_to(m, j, j).wait_recv())
+    for m in range(2):
+        each_other(z, y, k, lambda j: result_to(m, j, k).wait_send())
+
+
+def unpack_kernel(early_in, got, early, out):
+    early[...] = early_in[...]
+    for m in range(2):
+        for j in range(LANE):
+            whole = got[m, j].astype(F32)[0:24]
+            for o in range(2):
+                upper, lower = (
+                    pltpu.roll(whole, (128 - 32 * (2 * o + half)) % 128, 1)[:, 0:32] if 2 * o + half else whole[:, 0:32]
+                    for half in range(2)
+                )
                 for c in range(3):
-                    out[o, m, j, c] = one[16 * c : 16 * c + 16]
-    each_other(z, y, k, lambda j: result_to(j, k).wait_send())
+                    both = jnp.concatenate([upper[8 * c : 8 * c + 8], lower[8 * c : 8 * c + 8]], axis=0)
+                    out[o, m, j, c] = both.astype(BF16)
 
 
 def shards(
@@ -519,11 +526,11 @@
     base_output, base_head, upscale_input, upscale_time, upscale_gain, upscale_conv,
     upscale_query, upscale_output, upscale_head,
 ):
-    early, final_states = pl.pallas_call(
+    early, got = pl.pallas_call(
         step_kernel,
         out_shape=(
             jax.ShapeDtypeStruct((2, 3, 2, 256), BF16),
-            jax.ShapeDtypeStruct((2, 2, LANE, 3, 16, 32), BF16),
+            jax.ShapeDtypeStruct((2, LANE, 32, 128), BF16),
         ),
         in_specs=[SMEM] + [VMEM] * 10 + [ANY] * 12,
         out_specs=(VMEM, VMEM),
@@ -531,7 +538,7 @@
             pltpu.VMEM((256, 4096), BF16),
             pltpu.VMEM((3, 4096, 512), BF16),
             pltpu.VMEM((512, 512), BF16),
-            pltpu.VMEM((3, 1536, 512), BF16),
+            pltpu.VMEM((4608, 512), BF16),
             pltpu.VMEM((512, 512), BF16),
             pltpu.VMEM((512, 512), BF16),
             pltpu.VMEM((2, 128, 128), BF16),
@@ -541,7 +548,7 @@
             pltpu.VMEM((2, LANE, 3, 16, 32), BF16),
             pltpu.VMEM((256, 4096), BF16),
             pltpu.VMEM((256, 1536), BF16),
-            pltpu.VMEM((3, 640, 1536), BF16),
+            pltpu.VMEM((640, 4608), BF16),
             pltpu.VMEM((640, 512), F32),
             pltpu.VMEM((640, 512), BF16),
             pltpu.VMEM((640, 512), BF16),
@@ -560,21 +567,20 @@
             pltpu.VMEM((2, 128, 128), F32),
             pltpu.VMEM((8, 512), F32),
             pltpu.VMEM((2, 272, 128), F32),
-            pltpu.VMEM((34, 128, 128), F32),
-            pltpu.VMEM((34, 384, 128), BF16),
+            pltpu.VMEM((2, 34, 128, 128), F32),
+            pltpu.VMEM((2, 34, 384, 128), BF16),
             pltpu.VMEM((2, 2, 256, 128), F32),
             pltpu.VMEM((2, 3, 2, 256), F32),
             pltpu.VMEM((LANE, 32, 128), F32),
             pltpu.VMEM((LANE, 32, 128), BF16),
             pltpu.VMEM((LANE + 2, 32, 128), BF16),
-            pltpu.VMEM((LANE, 48, 128), BF16),
-            pltpu.VMEM((LANE, 48, 128), BF16),
+            pltpu.VMEM((2, LANE, 32, 128), BF16),
             pltpu.SemaphoreType.DMA((14,)),
             pltpu.SemaphoreType.DMA((LANE,)),
             pltpu.SemaphoreType.DMA((LANE + 2,)),
             pltpu.SemaphoreType.DMA((LANE,)),
-            pltpu.SemaphoreType.DMA((LANE,)),
-            pltpu.SemaphoreType.DMA((LANE,)),
+            pltpu.SemaphoreType.DMA((2, LANE)),
+            pltpu.SemaphoreType.DMA((2, LANE)),
         ],
         compiler_params=pltpu.CompilerParams(
             vmem_limit_bytes=56 * 1024 * 1024, collective_id=0, has_side_effects=True
@@ -584,9 +590,20 @@
         step_ids.T, token_ids, base_noise[:, 0].transpose(1, 0, 2), upscale_noise[:, 0].transpose(1, 0, 2), t5_gain[None],
         base_input, base_gain, base_head.T, upscale_input.transpose(1, 0, 2), upscale_gain.transpose(1, 0, 2),
         upscale_head.transpose(2, 0, 1), final_noise,
-        text_states.reshape(256, 4096), base_keyval, upscale_keyval, base_time, base_conv.reshape(3, 1536, 512),
+        text_states.reshape(256, 4096), base_keyval, upscale_keyval, base_time, base_conv.reshape(4608, 512),
         base_query, base_output, upscale_time, upscale_conv, upscale_query, upscale_output,
     )
+    early, final_states = pl.pallas_call(
+        unpack_kernel,
+        out_shape=(
+            jax.ShapeDtypeStruct((2, 3, 2, 256), BF16),
+            jax.ShapeDtypeStruct((2, 2, LANE, 3, 16, 32), BF16),
+        ),
+        in_specs=[VMEM] * 2,
+        out_specs=(VMEM, VMEM),
+        compiler_params=pltpu.CompilerParams(vmem_limit_bytes=8 * 1024 * 1024),
+        name="unpack",
+    )(early, got)
     return early.transpose(0, 2, 1, 3)[:, :, None], final_states
 
 

time: 47.6 us -> 41.8 us (0.88)
  Pallas kernels: 43.6 us -> 39.3 us
  local copies, waits for them, and re-layouts: 3.06 us -> 1.59 us
    pallas_call x1, Pallas kernels: 43.6 us -> 38.4 us  [shards(): pl.pallas_call(step_kernel, out_shape=(jax.ShapeDtypeStruct((2, 3, 2, 256...]
    unnamed x2 -> x4, local copies, waits for them, and re-layouts: 3.06 us -> 1.59 us
    pallas_call x0 -> x1, Pallas kernels: none -> 0.89 us  [shards(): pl.pallas_call(unpack_kernel, out_shape=(jax.ShapeDtypeStruct((2, 3, 2, 2...]
where the time goes in v2:
time: 41.8 us; the launch traced here: 41.5 us
  Pallas kernels  39.3 us (94%)
  local copies, waits for them, and re-layouts  1.59 us (4%)
  between operations  0.66 us (2%)
    pallas_call x1, Pallas kernels, shards(): pl.pallas_call(step_kernel, out_shape=(jax.ShapeDtypeStruct((2, 3, 2, 256...  38.4 us
    unnamed x4, local copies, waits for them, and re-layouts  1.59 us
    pallas_call x1, Pallas kernels, shards(): pl.pallas_call(unpack_kernel, out_shape=(jax.ShapeDtypeStruct((2, 3, 2, 2...  0.89 us

profile of v2, /device:TPU:17, one launch (start us, length us, event | category | flops | bytes accessed | tf_op | source)
XLA Modules:
  0.0 41.5 jit_solution(8480162400114921911)
XLA Ops:
  0.6 38.4 %denoise.1 = (bf16[2,3,2,256]{3,2,1,0:T(2,128)(2,1)}, bf16[2,8,32,128]{3,2,1,0:T(8,128)(2,1)}) custom-call(s32[2,3]{1,0:T(2,128)} %bitcast.28, s32[2,32,128]{2,1,0:T(8,128)} %ids.1, bf16[3,2,1024]{2,1,0:T(2,128)(2,1)} %bitcast.22, bf16[3,2,1024]{2,1,0:T(2,128)(2,1)} %bitcast.23, f32[1,4096]{1,0:T(1,128)} %bitcast.21, bf16[3,512]{1,0:T(4,128)(2,1)} %b_in.1, ...), custom_call_target="tpu_custom_call" | custom-call | tf_op jit(solution)/shard_map/denoise/pallas_call | solution.py:529
  39.0 0.0 copy-start
  39.0 0.9 %copy-done = bf16[2,8,32,128]{3,2,1,0:T(8,128)(2,1)S(1)} copy-done((bf16[2,8,32,128]{3,2,1,0:T(8,128)(2,1)S(1)}, bf16[2,8,32,128]{3,2,1,0:T(8,128)(2,1)}, u32[]{:S(2)}) %copy-start) | copy-done | bytes 131096
  39.9 0.0 copy-start.1
  39.9 0.7 %copy-done.1 = bf16[2,3,2,256]{3,2,1,0:T(2,128)(2,1)S(1)} copy-done((bf16[2,3,2,256]{3,2,1,0:T(2,128)(2,1)S(1)}, bf16[2,3,2,256]{3,2,1,0:T(2,128)(2,1)}, u32[]{:S(2)}) %copy-start.1) | copy-done | bytes 6168
  40.6 0.9 %unpack.1 = (bf16[2,3,2,256]{3,2,1,0:T(2,128)(2,1)}, bf16[2,2,8,3,16,32]{5,4,3,2,1,0:T(8,128)(2,1)}) custom-call(bf16[2,3,2,256]{3,2,1,0:T(2,128)(2,1)S(1)} %copy-done.1, bf16[2,8,32,128]{3,2,1,0:T(8,128)(2,1)S(1)} %copy-done), custom_call_target="tpu_custom_call" | custom-call | tf_op jit(solution)/shard_map/unpack/pallas_call | solution.py:596
Async XLA Ops:
  39.0 0.9 %copy-start = (bf16[2,8,32,128]{3,2,1,0:T(8,128)(2,1)S(1)}, bf16[2,8,32,128]{3,2,1,0:T(8,128)(2,1)}, u32[]{:S(2)}) copy-start(bf16[2,8,32,128]{3,2,1,0:T(8,128)(2,1)} %get-tuple-element.7.got) | copy-start | bytes 393220
  39.9 0.7 %copy-start.1 = (bf16[2,3,2,256]{3,2,1,0:T(2,128)(2,1)S(1)}, bf16[2,3,2,256]{3,2,1,0:T(2,128)(2,1)}, u32[]{:S(2)}) copy-start(bf16[2,3,2,256]{3,2,1,0:T(2,128)(2,1)} %get-tuple-element.6.early_in) | copy-start | bytes 18436

commit v3 on v2

--- a/solution.py
+++ b/solution.py
@@ -82,9 +82,8 @@
         pltpu.make_async_copy(src, dst, sems.at[n])
         for n, (src, dst) in enumerate(
             [
-                (noise_h.at[:, pl.ds(z * LANE, LANE)], noise_v),
                 (utime_h, utime_v), (uq_h, uq_v), (uo_h, uo_v), (uconv_h, uconv_v), (btime_h, btime_v),
-                (text_h, text_v), (bconv_h, bconv_v),
+                (text_h, text_v), (noise_h.at[:, pl.ds(z * LANE, LANE)], noise_v), (bconv_h, bconv_v),
             ]
             + [(bkv_h.at[:, 512 * n : 512 * n + 512], kv_w.at[n]) for n in range(2)]
             + [(ukv_h.at[n], kv_w.at[2, :, 256 * n : 256 * n + 256]) for n in range(2)]
@@ -93,41 +92,7 @@
     ]
     for copy in copies:
         copy.start()
-    at = dict(noise=0, utime=1, uq=2, uo=3, uconv=4, btime=5, text=6, bconv=7, kv=8, bq=12, bo=13)
-
-    copies[at["noise"]].wait()
-    packed = jnp.zeros((LANE * 24, 128), F32)
-    for m in range(2):
-        rows = noise_v[m].astype(F32)
-        for half in range(2):
-            group = 2 * m + half
-            place_at = (iota((32, 128), 0) + 32 * group == iota((32, 128), 1)).astype(F32).astype(BF16)
-            packed += dot(rows[:, :, 8 * half : 8 * half + 8, :].reshape(LANE * 24, 32).astype(BF16), place_at)
-    snd[:, 0:24, :] = packed.reshape(LANE, 24, 128)
-    snd[:, 24:32, :] = jnp.zeros((LANE, 8, 128), F32)
-    snd_b[...] = snd[...].astype(BF16)
-
-    lower = (k == LANE - 1) & (y < SEG - 1)
-    upper = (k == 0) & (y > 0)
-    extra = jnp.where(lower | upper, LANE, 0)
-    pl.semaphore_wait(barrier, LANE - 1 + jnp.where(y != z, 1, 0) + extra)
-
-    def noise_to(j, slot):
-        return remote(snd_b.at[j], rcv.at[slot], send.at[j], recv.at[slot], y, z * LANE + j)
-
-    def halo_to(j, slot, to):
-        return remote(snd_b.at[j], rcv.at[slot], halo_send.at[j], recv.at[slot], to, z * LANE + j)
-
-    each_other(z, y, k, lambda j: noise_to(j, k).start())
-    for cond, slot, step in ((lower, LANE, 1), (upper, LANE + 1, -1)):
-        @pl.when(cond)
-        def _():
-            for j in range(LANE):
-                halo_to(j, slot, y + step).start()
-
-    @pl.when(y == z)
-    def _():
-        rcv[k] = snd_b[k]
+    at = dict(utime=0, uq=1, uo=2, uconv=3, btime=4, text=5, noise=6, bconv=7, kv=8, bq=12, bo=13)
 
     lane128 = iota((128, 128), 1)
     sub128 = iota((128, 128), 0)
@@ -166,7 +131,7 @@
         level, earlier = alpha(step), alpha(step - 50.0)
         return jnp.sqrt(1.0 - level), 1.0 / jnp.sqrt(level), jnp.sqrt(earlier), jnp.sqrt(1.0 - earlier)
 
-    for n in range(1, 5):
+    for n in range(4):
         copies[n].wait()
     code_up = code(128, 1)
     code_base = code(512, 0)
@@ -234,17 +199,48 @@
 
     copies[at["text"]].wait()
 
-    def norm_step(i, carry):
-        at_row = pl.multiple_of(i * 64, 64)
-        states = text_v[pl.ds(at_row, 64), :].astype(F32)
+    copies[at["bconv"]].wait()
+
+    for i in range(4):
+        states = text_v[64 * i : 64 * i + 64, :].astype(F32)
         scale = lax.rsqrt(jnp.mean(states * states, axis=-1, keepdims=True) + 1e-6)
-        ctx[pl.ds(at_row, 64), :] = (states * scale * t5g[...]).astype(BF16)
-        return carry
-
-    lax.fori_loop(0, 4, norm_step, 0)
-    copies[at["bconv"]].wait()
+        ctx[64 * i : 64 * i + 64, :] = (states * scale * t5g[...]).astype(BF16)
 
     hid[...] += dot(taps[...], bconv_v[...])
+
+    copies[at["noise"]].wait()
+    packed = jnp.zeros((LANE * 24, 128), F32)
+    for m in range(2):
+        rows = noise_v[m].astype(F32)
+        for half in range(2):
+            group = 2 * m + half
+            place_at = (iota((32, 128), 0) + 32 * group == iota((32, 128), 1)).astype(F32).astype(BF16)
+            packed += dot(rows[:, :, 8 * half : 8 * half + 8, :].reshape(LANE * 24, 32).astype(BF16), place_at)
+    snd[:, 0:24, :] = packed.reshape(LANE, 24, 128)
+    snd[:, 24:32, :] = jnp.zeros((LANE, 8, 128), F32)
+    snd_b[...] = snd[...].astype(BF16)
+
+    lower = (k == LANE - 1) & (y < SEG - 1)
+    upper = (k == 0) & (y > 0)
+    extra = jnp.where(lower | upper, LANE, 0)
+    pl.semaphore_wait(barrier, LANE - 1 + jnp.where(y != z, 1, 0) + extra)
+
+    def noise_to(j, slot):
+        return remote(snd_b.at[j], rcv.at[slot], send.at[j], recv.at[slot], y, z * LANE + j)
+
+    def halo_to(j, slot, to):
+        return remote(snd_b.at[j], rcv.at[slot], halo_send.at[j], recv.at[slot], to, z * LANE + j)
+
+    each_other(z, y, k, lambda j: noise_to(j, k).start())
+    for cond, slot, step in ((lower, LANE, 1), (upper, LANE + 1, -1)):
+        @pl.when(cond)
+        def _():
+            for j in range(LANE):
+                halo_to(j, slot, y + step).start()
+
+    @pl.when(y == z)
+    def _():
+        rcv[k] = snd_b[k]
 
     for n in range(3):
         copies[at["kv"] + n].wait()
@@ -601,7 +597,7 @@
         ),
         in_specs=[VMEM] * 2,
         out_specs=(VMEM, VMEM),
-        compiler_params=pltpu.CompilerParams(vmem_limit_bytes=8 * 1024 * 1024),
+        compiler_params=pltpu.CompilerParams(vmem_limit_bytes=60 * 1024 * 1024),
         name="unpack",
     )(early, got)
     return early.transpose(0, 2, 1, 3)[:, :, None], final_states

time: 41.8 us -> 38.1 us (0.911)
  Pallas kernels: 39.3 us -> 37.3 us
  local copies, waits for them, and re-layouts: 1.59 us -> 0 us
    pallas_call x1, Pallas kernels: 38.4 us -> 35.5 us  [shards(): pl.pallas_call(step_kernel, out_shape=(jax.ShapeDtypeStruct((2, 3, 2, 256...]
    unnamed x4 -> x0, local copies, waits for them, and re-layouts: 1.59 us -> none
    pallas_call x1, Pallas kernels: 0.89 us -> 1.82 us  [shards(): pl.pallas_call(unpack_kernel, out_shape=(jax.ShapeDtypeStruct((2, 3, 2, 2...]
where the time goes in v3:
time: 38.1 us; the launch traced here: 37.9 us
  Pallas kernels  37.3 us (98%)
  between operations  0.65 us (2%)
    pallas_call x1, Pallas kernels, shards(): pl.pallas_call(step_kernel, out_shape=(jax.ShapeDtypeStruct((2, 3, 2, 256...  35.5 us
    pallas_call x1, Pallas kernels, shards(): pl.pallas_call(unpack_kernel, out_shape=(jax.ShapeDtypeStruct((2, 3, 2, 2...  1.82 us

profile of v3, /device:TPU:17, one launch (start us, length us, event | category | flops | bytes accessed | tf_op | source)
XLA Modules:
  0.0 37.9 jit_solution(3833411210445897554)
XLA Ops:
  0.6 35.5 %denoise.1 = (bf16[2,3,2,256]{3,2,1,0:T(2,128)(2,1)}, bf16[2,8,32,128]{3,2,1,0:T(8,128)(2,1)}) custom-call(s32[2,3]{1,0:T(2,128)} %bitcast.28, s32[2,32,128]{2,1,0:T(8,128)} %ids.1, bf16[3,2,1024]{2,1,0:T(2,128)(2,1)} %bitcast.22, bf16[3,2,1024]{2,1,0:T(2,128)(2,1)} %bitcast.23, f32[1,4096]{1,0:T(1,128)} %bitcast.21, bf16[3,512]{1,0:T(4,128)(2,1)} %b_in.1, ...), custom_call_target="tpu_custom_call" | custom-call | tf_op jit(solution)/shard_map/denoise/pallas_call | solution.py:525
  36.1 1.8 %unpack.1 = (bf16[2,3,2,256]{3,2,1,0:T(2,128)(2,1)}, bf16[2,2,8,3,16,32]{5,4,3,2,1,0:T(8,128)(2,1)}) custom-call(bf16[2,3,2,256]{3,2,1,0:T(2,128)(2,1)} %get-tuple-element.6.early_in, bf16[2,8,32,128]{3,2,1,0:T(8,128)(2,1)} %get-tuple-element.7.got), custom_call_target="tpu_custom_call" | custom-call | tf_op jit(solution)/shard_map/unpack/pallas_call | solution.py:592

commit v4 on v3

--- a/solution.py
+++ b/solution.py
@@ -58,7 +58,7 @@
     text_v, kv_w, btime_v, bconv_v, bq_v, bo_v, utime_v, uconv_v, uq_v, uo_v, noise_v,
     ctx, kv, taps, hid, query, att, x8b, x8u, rows8, aug8, gcol, wq_t, wo_t, wh_t, conv_t,
     kcat, vcat, mask_row, mask_col, head8, x2, hid3, act3, c2, early_v,
-    snd, snd_b, rcv, snd2, sems, send, recv, halo_send, send2, recv2,
+    snd, snd_b, rcv, snd2, sems, send, recv, halo_send, send2, recv2, own_sems,
 ):
     z, y, k = place()
     p = y * LANE + k
@@ -83,8 +83,9 @@
         for n, (src, dst) in enumerate(
             [
                 (utime_h, utime_v), (uq_h, uq_v), (uo_h, uo_v), (uconv_h, uconv_v), (btime_h, btime_v),
-                (text_h, text_v), (noise_h.at[:, pl.ds(z * LANE, LANE)], noise_v), (bconv_h, bconv_v),
+                (text_h, text_v), (noise_h.at[:, pl.ds(z * LANE, LANE)], noise_v),
             ]
+            + [(bconv_h.at[1536 * n : 1536 * n + 1536], bconv_v.at[1536 * n : 1536 * n + 1536]) for n in range(3)]
             + [(bkv_h.at[:, 512 * n : 512 * n + 512], kv_w.at[n]) for n in range(2)]
             + [(ukv_h.at[n], kv_w.at[2, :, 256 * n : 256 * n + 256]) for n in range(2)]
             + [(bq_h, bq_v), (bo_h, bo_v)]
@@ -92,7 +93,7 @@
     ]
     for copy in copies:
         copy.start()
-    at = dict(utime=0, uq=1, uo=2, uconv=3, btime=4, text=5, noise=6, bconv=7, kv=8, bq=12, bo=13)
+    at = dict(utime=0, uq=1, uo=2, uconv=3, btime=4, text=5, noise=6, bconv=7, kv=10, bq=14, bo=15)
 
     lane128 = iota((128, 128), 1)
     sub128 = iota((128, 128), 0)
@@ -199,14 +200,14 @@
 
     copies[at["text"]].wait()
 
-    copies[at["bconv"]].wait()
-
     for i in range(4):
         states = text_v[64 * i : 64 * i + 64, :].astype(F32)
         scale = lax.rsqrt(jnp.mean(states * states, axis=-1, keepdims=True) + 1e-6)
         ctx[64 * i : 64 * i + 64, :] = (states * scale * t5g[...]).astype(BF16)
 
-    hid[...] += dot(taps[...], bconv_v[...])
+    for n in range(3):
+        copies[at["bconv"] + n].wait()
+        hid[...] += dot(taps[:, 1536 * n : 1536 * n + 1536], bconv_v[1536 * n : 1536 * n + 1536, :])
 
     copies[at["noise"]].wait()
     packed = jnp.zeros((LANE * 24, 128), F32)
@@ -392,7 +393,8 @@
             x2[m, 3 + c : 4 + c, :] = above[c : c + 1]
             x2[m, 33 * 8 + 3 + c : 33 * 8 + 4 + c, :] = below[c : c + 1]
 
-    early[...] = early_v[...].astype(BF16)
+    early_out = pltpu.make_async_copy(early_v, early, own_sems.at[2])
+    early_out.start()
     each_other(z, y, k, lambda j: noise_to(j, j).wait_recv())
 
     @pl.when(z > 0)
@@ -434,6 +436,9 @@
     def result_to(m, j, slot):
         return remote(snd2.at[m, j], rcv2.at[m, slot], send2.at[m, j], recv2.at[m, slot], y, z * LANE + j)
 
+    def own_to(m):
+        return pltpu.make_async_copy(snd2.at[m, k], rcv2.at[m, k], own_sems.at[m])
+
     FT = 17
     lanef = iota((1, 128 * FT), 1)
     colf = iota((1, 128), 1) & 31
@@ -486,7 +491,7 @@
 
         @pl.when(y == z)
         def _():
-            rcv2[m, k] = snd2[m, k]
+            own_to(m).start()
 
     each_other(z, y, k, lambda j: noise_to(j, k).wait_send())
     for cond, slot, step in ((lower, LANE, 1), (upper, LANE + 1, -1)):
@@ -500,10 +505,17 @@
     for m in range(2):
         each_other(z, y, k, lambda j: result_to(m, j, k).wait_send())
 
+    @pl.when(y == z)
+    def _():
+        for m in range(2):
+            own_to(m).wait()
+
+    early_out.wait()
+
 
 def unpack_kernel(early_in, got, early, out):
-    early[...] = early_in[...]
-    for m in range(2):
+    early[...] = early_in[...].astype(BF16)
+    for m in range(1):
         for j in range(LANE):
             whole = got[m, j].astype(F32)[0:24]
             for o in range(2):
@@ -525,11 +537,11 @@
     early, got = pl.pallas_call(
         step_kernel,
         out_shape=(
-            jax.ShapeDtypeStruct((2, 3, 2, 256), BF16),
+            jax.ShapeDtypeStruct((2, 3, 2, 256), F32),
             jax.ShapeDtypeStruct((2, LANE, 32, 128), BF16),
         ),
         in_specs=[SMEM] + [VMEM] * 10 + [ANY] * 12,
-        out_specs=(VMEM, VMEM),
+        out_specs=(ANY, ANY),
         scratch_shapes=[
             pltpu.VMEM((256, 4096), BF16),
             pltpu.VMEM((3, 4096, 512), BF16),
@@ -571,12 +583,13 @@
             pltpu.VMEM((LANE, 32, 128), BF16),
             pltpu.VMEM((LANE + 2, 32, 128), BF16),
             pltpu.VMEM((2, LANE, 32, 128), BF16),
-            pltpu.SemaphoreType.DMA((14,)),
+            pltpu.SemaphoreType.DMA((16,)),
             pltpu.SemaphoreType.DMA((LANE,)),
             pltpu.SemaphoreType.DMA((LANE + 2,)),
             pltpu.SemaphoreType.DMA((LANE,)),
             pltpu.SemaphoreType.DMA((2, LANE)),
             pltpu.SemaphoreType.DMA((2, LANE)),
+            pltpu.SemaphoreType.DMA((3,)),
         ],
         compiler_params=pltpu.CompilerParams(
             vmem_limit_bytes=56 * 1024 * 1024, collective_id=0, has_side_effects=True
@@ -595,8 +608,15 @@
             jax.ShapeDtypeStruct((2, 3, 2, 256), BF16),
             jax.ShapeDtypeStruct((2, 2, LANE, 3, 16, 32), BF16),
         ),
-        in_specs=[VMEM] * 2,
-        out_specs=(VMEM, VMEM),
+        grid=(2,),
+        in_specs=[
+            pl.BlockSpec((2, 3, 2, 256), lambda m: (0, 0, 0, 0)),
+            pl.BlockSpec((1, LANE, 32, 128), lambda m: (m, 0, 0, 0)),
+        ],
+        out_specs=(
+            pl.BlockSpec((2, 3, 2, 256), lambda m: (0, 0, 0, 0)),
+            pl.BlockSpec((2, 1, LANE, 3, 16, 32), lambda m: (0, m, 0, 0, 0, 0)),
+        ),
         compiler_params=pltpu.CompilerParams(vmem_limit_bytes=60 * 1024 * 1024),
         name="unpack",
     )(early, got)

time: 38.1 us -> 37.8 us (level)
  Pallas kernels: 37.3 us -> 36.9 us
where the time goes in v4:
time: 37.8 us; the launch traced here: 37.5 us
  Pallas kernels  36.9 us (98%)
  between operations  0.65 us (2%)
    pallas_call x1, Pallas kernels, shards(): pl.pallas_call(step_kernel, out_shape=(jax.ShapeDtypeStruct((2, 3, 2, 256...  35.1 us
    pallas_call x1, Pallas kernels, shards(): pl.pallas_call(unpack_kernel, out_shape=(jax.ShapeDtypeStruct((2, 3, 2, 2...  1.77 us

profile of v4, /device:TPU:17, one launch (start us, length us, event | category | flops | bytes accessed | tf_op | source)
XLA Modules:
  0.0 37.5 jit_solution(10526396922449160824)
XLA Ops:
  0.6 35.1 %denoise.1 = (f32[2,3,2,256]{3,2,1,0:T(2,128)}, bf16[2,8,32,128]{3,2,1,0:T(8,128)(2,1)}) custom-call(s32[2,3]{1,0:T(2,128)} %bitcast.28, s32[2,32,128]{2,1,0:T(8,128)} %ids.1, bf16[3,2,1024]{2,1,0:T(2,128)(2,1)} %bitcast.22, bf16[3,2,1024]{2,1,0:T(2,128)(2,1)} %bitcast.23, f32[1,4096]{1,0:T(1,128)} %bitcast.21, bf16[3,512]{1,0:T(4,128)(2,1)} %b_in.1, ...), custom_call_target="tpu_custom_call" | custom-call | tf_op jit(solution)/shard_map/denoise/pallas_call | solution.py:537
  35.8 1.8 %unpack.1 = (bf16[2,3,2,256]{3,2,1,0:T(2,128)(2,1)}, bf16[2,2,8,3,16,32]{5,4,3,2,1,0:T(8,128)(2,1)}) custom-call(f32[2,3,2,256]{3,2,1,0:T(2,128)} %get-tuple-element.6.early_in, bf16[2,8,32,128]{3,2,1,0:T(8,128)(2,1)} %get-tuple-element.7.got), custom_call_target="tpu_custom_call" | custom-call | tf_op jit(solution)/shard_map/unpack/pallas_call | solution.py:605
